TPU v7x, 128 devices: a whole 4x4x4 slice. The times are simulated.
128 devices in a mesh: group: 4 (over x), dev: 32 (over y, z, core).
Axes of the slice: x: 4, y: 4, z: 4, core: 2. Of those that a mesh axis runs over, the one named last changes fastest.
Arguments:
- embeddings: bfloat16 [131072, 768], P(('group', 'dev'))
- labels: int32 [131072], P(('group', 'dev')), may hold values from 0 to 4095, as said below
- ranking: int32 [131072], P(('group', 'dev')), may hold values from 0 to 131071, each once
- send_list: int32 [128, 32], P(('group', 'dev')), may hold values from 0 to 3
- pair_list: int32 [128, 32], P(('group', 'dev')), may hold values from 0 to 3
Outputs:
- scores: float32 [131072], P(('group', 'dev'))
- centroids: float32 [4096, 768], P(('group', 'dev'))
Inputs may be any that keep to these rules, and one draw needn't show every extreme that they name: `labels`: every cluster holds at least one point, and cluster sizes are skewed. Within each group of 32 devices the points are sorted by cluster and laid out block by block: block k of the device with peer index d holds run number k * 32 + d of 256 points of the group in that order.
All inputs are finite; a program needn't handle non-finite values.
Results may differ from a plain program's by a relative error of at most 0.0003.
The roundings to bfloat16 on the way count: a program that leaves them out, or rounds other values in their place, can miss the bound.
Values may be sent and summed in bfloat16 or wider, within the bound.
A program may use at most 128 MiB of HBM per device.

v0:
```python
import jax
import jax.numpy as jnp
from jax import lax
from jax.sharding import PartitionSpec as P

K = 4096
BLOCK = 256


def make_unit(embeddings):
    values = embeddings.astype(jnp.float32)
    scaled = values * lax.rsqrt(jnp.sum(values * values, axis=-1, keepdims=True) + 1e-06)
    return scaled.astype(jnp.bfloat16)


def body(embeddings, labels, ranking, send_list, pair_list):
    unit_rows = make_unit(embeddings)
    point_count = unit_rows.shape[0]
    feature_count = unit_rows.shape[1]
    peer_count = lax.axis_size("dev")
    group_count = lax.axis_size("group")
    block_count = point_count // BLOCK
    step_rows = min(point_count, 2 * BLOCK)
    blocks = unit_rows.reshape(block_count, BLOCK, feature_count)
    block_labels = labels.reshape(block_count, BLOCK)
    block_ranks = ranking.reshape(block_count, BLOCK)
    sent_ids = send_list[0]
    paired_ids = pair_list[0]
    outgoing = (blocks[sent_ids], block_labels[sent_ids], block_ranks[sent_ids])
    arrived, arrived_labels, arrived_ranks = (
        lax.all_to_all(outgoing[0], "dev", split_axis=0, concat_axis=0, tiled=True),
        lax.all_to_all(outgoing[1], "dev", split_axis=0, concat_axis=0, tiled=True),
        lax.all_to_all(outgoing[2], "dev", split_axis=0, concat_axis=0, tiled=True),
    )

    def local_part(offset):
        row_block = lax.dynamic_slice_in_dim(unit_rows, offset, step_rows, 0)
        row_labels = lax.dynamic_slice_in_dim(labels, offset, step_rows, 0)
        row_ranks = lax.dynamic_slice_in_dim(ranking, offset, step_rows, 0)
        similar = jnp.dot(row_block, unit_rows.T, preferred_element_type=jnp.float32)
        allowed = (row_labels[:, None] == labels[None, :]) & (ranking[None, :] < row_ranks[:, None])
        return jnp.max(jnp.where(allowed, similar, -2.0), axis=1)

    starts = jnp.arange(point_count // step_rows, dtype=jnp.int32) * step_rows
    local_scores = lax.map(local_part, starts).reshape(point_count)
    mine_rows = blocks[paired_ids]
    mine_labels = block_labels[paired_ids]
    mine_ranks = block_ranks[paired_ids]
    similar = jnp.einsum("pjd,pid->pji", arrived, mine_rows, preferred_element_type=jnp.float32)
    same_label = arrived_labels[:, :, None] == mine_labels[:, None, :]
    arrived_later = same_label & (mine_ranks[:, None, :] < arrived_ranks[:, :, None])
    mine_later = same_label & (arrived_ranks[:, :, None] < mine_ranks[:, None, :])
    for_arrived = jnp.max(jnp.where(arrived_later, similar, -2.0), axis=2)
    for_mine = jnp.max(jnp.where(mine_later, similar, -2.0), axis=1)
    returned = lax.all_to_all(for_arrived, "dev", split_axis=0, concat_axis=0, tiled=True)
    block_ids = jnp.arange(block_count, dtype=jnp.int32)
    hit_mine = paired_ids[:, None] == block_ids[None, :]
    best_mine = jnp.max(jnp.where(hit_mine[:, :, None], for_mine[:, None, :], -2.0), axis=0)
    hit_sent = sent_ids[:, None] == block_ids[None, :]
    best_back = jnp.max(jnp.where(hit_sent[:, :, None], returned[:, None, :], -2.0), axis=0)
    tile_scores = jnp.maximum(best_mine, best_back).reshape(point_count)
    scores = jnp.maximum(jnp.maximum(local_scores, tile_scores), 0.0)
    cluster_share = K // (group_count * peer_count)
    cluster_ids = jnp.arange(lax.axis_size(("group", "dev")) * cluster_share, dtype=jnp.int32)
    indicator = (cluster_ids[:, None] == labels[None, :]).astype(jnp.bfloat16)
    totals = lax.psum_scatter(
        jnp.dot(indicator, unit_rows, preferred_element_type=jnp.float32),
        ("group", "dev"),
        scatter_dimension=0,
        tiled=True,
    )
    centroids = totals * lax.rsqrt(jnp.mean(totals * totals, axis=-1, keepdims=True) + 1e-06)
    return (scores, centroids)


def solution(mesh):
    return jax.shard_map(
        body,
        mesh=mesh,
        in_specs=(
            P(("group", "dev"), None),
            P(("group", "dev")),
            P(("group", "dev")),
            P(("group", "dev"), None),
            P(("group", "dev"), None),
        ),
        out_specs=(P(("group", "dev")), P(("group", "dev"), None)),
        check_vma=False,
    )
```

profile of v0, /device:TPU:0, one launch (start us, length us, event | category | flops | bytes accessed | tf_op | source)
XLA Modules:
  0.0 303.3 jit_solution(6912150887737920829)
XLA Ops:
  7.2 0.0 copy-start
  7.2 0.0 reduce-scatter.2.cloned.1.call-start
  7.2 1.8 fusion.4
  9.0 1.7 fusion.5
  10.8 0.0 copy-done
  10.8 11.5 %fusion.2 = f32[4096,768]{1,0:T(8,128)} fusion(bf16[1024,768]{1,0:T(8,128)(2,1)S(1)} %fusion.5, s32[1024]{0:T(1024)S(1)} %copy-done), kind=kOutput, calls=%fused_computation.10 | convolution fusion | flops 6446645248 | bytes 14159872 | tf_op jit(solution)/shard_map/dot_general | solution.py:67
  22.3 0.0 copy-start.1
  22.3 0.0 copy-start.2
  22.3 0.0 reduce-scatter.2.cloned.1.call-update
  22.3 0.7 copy-done.1
  23.0 0.0 copy-done.2
  23.0 0.6 gather_fusion.2
  23.6 0.6 copy.10
  24.2 8.4 %all-to-all-start.1 = ((s32[32,1,256]{2,1,0:T(1,128)}), s32[32,1,256]{2,1,0:T(1,128)S(1)}, u32[]{:S(2)}, u32[]{:S(2)}) async-start(s32[32,1,256]{2,1,0:T(1,128)} %copy.10), calls=%async_computation.1 | async-start | bytes 65536 | tf_op jit(solution)/shard_map/all_to_all | solution.py:33
  32.7 0.6 gather_fusion
  33.3 0.6 copy.9
  33.9 6.2 %all-to-all-done.1 = s32[32,1,256]{2,1,0:T(1,128)S(1)} async-done(((s32[32,1,256]{2,1,0:T(1,128)}), s32[32,1,256]{2,1,0:T(1,128)S(1)}, u32[]{:S(2)}, u32[]{:S(2)}) %all-to-all-start.1) | async-done | bytes 32800 | tf_op jit(solution)/shard_map/all_to_all | solution.py:33
  40.1 3.8 %all-to-all-start = ((s32[32,1,256]{2,1,0:T(1,128)}), s32[32,1,256]{2,1,0:T(1,128)S(1)}, u32[]{:S(2)}, u32[]{:S(2)}) async-start(s32[32,1,256]{2,1,0:T(1,128)} %copy.9), calls=%async_computation | async-start | bytes 65536 | tf_op jit(solution)/shard_map/all_to_all | solution.py:32
  43.9 6.8 %gather_fusion.4 = bf16[32,256,768]{2,1,0:T(8,128)(2,1)} fusion(bf16[4,256,768]{2,1,0:T(8,128)(2,1)S(1)} %bitcast.39, s32[1024]{0:T(1024)S(1)} %pad_clamp_fusion.1), kind=kCustom, calls=%fused_computation.4 | custom fusion | bytes 25165952 | tf_op jit(solution)/shard_map/gather | solution.py:29
  50.7 0.0 copy-start.3
  50.7 0.6 all-to-all-done
  51.3 6.8 %all-to-all-start.2 = ((bf16[32,256,768]{2,1,0:T(8,128)(2,1)}), bf16[32,256,768]{2,1,0:T(8,128)(2,1)}, u32[]{:S(2)}, u32[]{:S(2)}) async-start(bf16[32,256,768]{2,1,0:T(8,128)(2,1)} %gather_fusion.4), calls=%async_computation.2 | async-start | bytes 25165824 | tf_op jit(solution)/shard_map/all_to_all | solution.py:31
  58.1 0.0 copy-done.3
  58.2 6.8 %gather_fusion.5 = bf16[32,256,768]{2,1,0:T(8,128)(2,1)} fusion(bf16[4,256,768]{2,1,0:T(8,128)(2,1)S(1)} %bitcast.40, s32[1024]{0:T(1024)S(1)} %pad_clamp_fusion), kind=kCustom, calls=%fused_computation.5 | custom fusion | bytes 25165952 | tf_op jit(solution)/shard_map/gather | solution.py:46
  65.0 0.6 gather_fusion.1
  65.6 0.6 gather_fusion.3
  66.2 7.8 %while.10 = (s32[]{:T(128)}, f32[2,512]{1,0:T(2,128)S(1)}, s32[2]{0:T(128)S(1)}, s32[1024]{0:T(1024)S(1)}, s32[1024]{0:T(1024)S(1)}, /*index=5*/bf16[1024,768]{1,0:T(8,128)(2,1)S(1)}, s32[]{:T(128)}, s32[]{:T(128)}, s32[]{:T(128)}) while((s32[]{:T(128)}, f32[2,512]{1,0:T(2,128)S(1)}, s32[2]{0:T(128)S(1)}, s32[1024]{0:T(1024)S(1)}, ...), condition=%wide.region_3.4_spmd, body=%wide.region_1.3_spmd.sunk | while | flops 807927296 | bytes 2386075 | solution.py:45
  66.2 0.6 dynamic_slice.20
  68.7 0.1 dynamic_slice.21
  68.8 0.1 dynamic_slice.22
  68.9 1.2 select_reduce_fusion.6
  70.1 0.6 dynamic_slice.20
  72.7 0.1 dynamic_slice.21
  72.7 0.1 dynamic_slice.22
  72.8 1.2 select_reduce_fusion.6
  74.1 175.6 %all-to-all-done.2 = bf16[32,256,768]{2,1,0:T(8,128)(2,1)} async-done(((bf16[32,256,768]{2,1,0:T(8,128)(2,1)}), bf16[32,256,768]{2,1,0:T(8,128)(2,1)}, u32[]{:S(2)}, u32[]{:S(2)}) %all-to-all-start.2) | async-done | bytes 12582944 | tf_op jit(solution)/shard_map/all_to_all | solution.py:31
  249.6 11.3 %select_reduce_fusion.1 = (f32[32,256]{1,0:T(8,128)S(1)}, f32[32,256]{1,0:T(8,128)S(1)}) fusion(s32[32,256]{1,0:T(8,128)S(1)} %gather_fusion.3, s32[32,256]{1,0:T(8,128)S(1)} %bitcast.45, s32[32,256]{1,0:T(8,128)S(1)} %gather_fusion.1, s32[32,256]{1,0:T(8,128)S(1)} %bitcast.46, bf16[32,256,768]{2,1,0:T(8,128)(2,1)} %all-to-all-done.2, ...), kind=kOutput, calls=%fused_computation.14 | convolution fusion | flops 3240083456 | bytes 25362432 | tf_op jit(solution)/shard_map/pjd,pid->pji/dot_general | solution.py:49
  260.9 0.6 all_to_all.26
  261.5 24.1 %all-to-all-start.3 = ((f32[32,1,256]{2,1,0:T(1,128)}), f32[32,1,256]{2,1,0:T(1,128)S(1)}, u32[]{:S(2)}, u32[]{:S(2)}) async-start(f32[32,1,256]{2,1,0:T(1,128)} %all_to_all.26), calls=%async_computation.3 | async-start | bytes 65536 | tf_op jit(solution)/shard_map/all_to_all | solution.py:55
  285.6 0.1 select_reduce_fusion.4
  285.7 7.3 %all-to-all-done.3 = f32[32,1,256]{2,1,0:T(1,128)S(1)} async-done(((f32[32,1,256]{2,1,0:T(1,128)}), f32[32,1,256]{2,1,0:T(1,128)S(1)}, u32[]{:S(2)}, u32[]{:S(2)}) %all-to-all-start.3) | async-done | bytes 32800 | tf_op jit(solution)/shard_map/all_to_all | solution.py:55
  293.0 0.1 select_reduce_fusion.3
  293.2 0.6 maximum_maximum_fusion
  293.8 0.0 reduce-scatter.2.cloned.1.call-done
  293.8 1.0 multiply_reduce_fusion
  294.8 1.6 broadcast_multiply_fusion
  (20 shorter events, 0.2 us)
Async XLA Ops:
  7.2 3.6 %copy-start = (s32[1024]{0:T(1024)S(1)}, s32[1024]{0:T(1024)}, u32[]{:S(2)}) copy-start(s32[1024]{0:T(1024)} %param.8) | copy-start | bytes 12292
  7.2 286.6 %reduce-scatter.2.cloned.1.call-start = ((), (), s32[]{:S(2)}) async-start(), calls=%async_computation.5 | async-start | bytes 12681216 | tf_op jit(solution)/shard_map/reduce_scatter | solution.py:66
  22.3 0.7 copy-start.1
  22.3 0.7 copy-start.2
  24.2 15.9 %all-to-all-start.1 = ((s32[32,1,256]{2,1,0:T(1,128)}), s32[32,1,256]{2,1,0:T(1,128)S(1)}, u32[]{:S(2)}, u32[]{:S(2)}) async-start(s32[32,1,256]{2,1,0:T(1,128)} %copy.10), calls=%async_computation.1 | async-start | bytes 65536 | tf_op jit(solution)/shard_map/all_to_all | solution.py:33
  40.1 11.2 %all-to-all-start = ((s32[32,1,256]{2,1,0:T(1,128)}), s32[32,1,256]{2,1,0:T(1,128)S(1)}, u32[]{:S(2)}, u32[]{:S(2)}) async-start(s32[32,1,256]{2,1,0:T(1,128)} %copy.9), calls=%async_computation | async-start | bytes 65536 | tf_op jit(solution)/shard_map/all_to_all | solution.py:32
  50.7 7.4 %copy-start.3 = (s32[1,32]{1,0:T(1,128)S(1)}, s32[1,32]{1,0:T(1,128)}, u32[]{:S(2)}) copy-start(s32[1,32]{1,0:T(1,128)} %param.11) | copy-start | bytes 388
  51.3 198.3 %all-to-all-start.2 = ((bf16[32,256,768]{2,1,0:T(8,128)(2,1)}), bf16[32,256,768]{2,1,0:T(8,128)(2,1)}, u32[]{:S(2)}, u32[]{:S(2)}) async-start(bf16[32,256,768]{2,1,0:T(8,128)(2,1)} %gather_fusion.4), calls=%async_computation.2 | async-start | bytes 25165824 | tf_op jit(solution)/shard_map/all_to_all | solution.py:31
  261.5 31.5 %all-to-all-start.3 = ((f32[32,1,256]{2,1,0:T(1,128)}), f32[32,1,256]{2,1,0:T(1,128)S(1)}, u32[]{:S(2)}, u32[]{:S(2)}) async-start(f32[32,1,256]{2,1,0:T(1,128)} %all_to_all.26), calls=%async_computation.3 | async-start | bytes 65536 | tf_op jit(solution)/shard_map/all_to_all | solution.py:55
Sparse Core Ops, SparseCore 0:
  22.4 256.8 reduce-scatter.1
where the time goes:
time: 305 us; the launch traced here: 303 us
  waiting for transfers between devices  190 us (62%)
  starting transfers between devices  43.1 us (14%)
  matrix products  25.1 us (8%)
  local copies, waits for them, and re-layouts  20.2 us (7%)
  between operations  14.2 us (5%)
  other arithmetic  6.99 us (2%)
  loops' own time  3.93 us (1%)
    all_to_all x1, waiting for transfers between devices, body(): lax.all_to_all(outgoing[0], 'dev', split_axis=0, concat_axis=0, tiled=True)  176 us
    all_to_all x1, starting transfers between devices, body(): lax.all_to_all(for_arrived, 'dev', split_axis=0, concat_axis=0, tiled=True)  24.1 us
    dot_general x1, matrix products, body(): jnp.dot(indicator, unit_rows, preferred_element_type=jnp.float32)  11.5 us
    dot_general x1, matrix products, body(): jnp.einsum('pjd,pid->pji', arrived, mine_rows, preferred_element_type=jnp...  11.3 us
    all_to_all x1, starting transfers between devices, body(): lax.all_to_all(outgoing[2], 'dev', split_axis=0, concat_axis=0, tiled=True)  8.41 us
    gather x3, local copies, waits for them, and re-layouts, body(): outgoing = (blocks[sent_ids], block_labels[sent_ids], block_ranks[sent_ids])  8.01 us
    all_to_all x1, waiting for transfers between devices, body(): lax.all_to_all(for_arrived, 'dev', split_axis=0, concat_axis=0, tiled=True)  7.33 us
    all_to_all x1, starting transfers between devices, body(): lax.all_to_all(outgoing[0], 'dev', split_axis=0, concat_axis=0, tiled=True)  6.81 us
  transfers between devices with their start and end apart: 5, of which 4 were waited for; matrix products, arithmetic and copies ran while one was open for 11% of the time, Pallas kernels for 0%

commit v1 on v0

v1 whole, which is shorter than its diff:
```python
import jax
import jax.numpy as jnp
from jax import lax
from jax.experimental import pallas as pl
from jax.experimental.pallas import tpu as pltpu
from jax.sharding import PartitionSpec as P

K = 4096
BLOCK = 256
ROWS = 1024
SLICES = 6
LANES = 128
LOW = -2.0
MESH = pl.DeviceIdType.MESH
M1, M2, M3, X1, X2, P0, P1, P2, P3 = range(9)
QUEUE = [("o", 0), ("o", 1), ("o", 2), ("o", 3), ("f", 0), ("f", 1), ("f", 2), ("f", 3), ("o", 4), ("o", 5), ("f", 4), ("f", 5),
         ("g", 0), ("g", 1), ("g", 2)]
ARRIVES = {"o": M1, "f": M2, "g": M3}


def pick(j, values):
    out = values[3]
    for i in (2, 1, 0):
        out = jnp.where(j == i, values[i], out)
    return out


def slice_id(j, n):
    pair = pick(j, ((2, 0, 1, 2), (0, 1, 0, 1), (1, 2, 2, 0))[n // 2])
    return pair * 2 + n % 2


def kernel(emb, lab_in, rank_in, send_in, pair_in, scores_out,
           own, m1, m2, m3, x1, x2, p0, p1, p2, p3,
           own_meta, *rest):
    metas = rest[0:9]
    lists = rest[9:19]
    cols = rest[19:27]
    accs = rest[27:37]
    flats = rest[37:47]
    (result_in, q_send, q_recv, fwd_send, fwd_recv, e_send, e_recv, d_send, d_recv, meta_send, meta_recv, list_sem,
     res_send, res_recv) = rest[47:]
    bufs = (m1, m2, m3, x1, x2, p0, p1, p2, p3)
    group = lax.axis_index("group")
    me = lax.axis_index("dev")
    core = lax.rem(me, 2)
    y, z = me // 8, lax.rem(me // 2, 4)
    main = jnp.where(core == 0, z, y)
    side = jnp.where(core == 0, y, z)
    phase = lax.rem(y + z, 4)

    def place(u, w, e):
        return lax.rem(u, 4) * (2 + 6 * e) + lax.rem(w, 4) * (8 - 6 * e) + e

    def at(index):
        return (group, index)

    other = 1 - core
    sources = [place(main + 1, side, core), place(main + 2, side, core), place(main + 3, side, core),
               place(main, side + 3, core), place(main, side + 2, core),
               place(side, main, other), place(side + 1, main, other), place(side + 2, main, other), place(side + 3, main, other)]
    holders = [place(main + 3, side, core), place(main + 2, side, core), place(main + 1, side, core),
               place(main, side + 1, core), place(main, side + 2, core),
               place(side, main, other), place(side, main + 3, other), place(side, main + 2, other), place(side, main + 1, other)]
    back = at(place(main + 3, side, core))
    forth = at(place(main + 1, side, core))
    along = at(place(main, side + 1, core))
    partner = at(place(side, main, other))

    barrier = pltpu.get_barrier_semaphore()

    def greet(i, carry):
        pl.semaphore_signal(barrier, inc=1, device_id=at(lax.rem(me + i, 32)), device_id_type=MESH)
        return carry

    lax.fori_loop(1, 32, greet, 0)

    own_meta[0:8, :] = lab_in[...]
    own_meta[8:16, :] = rank_in[...]
    own_meta[16:17, 0:32] = send_in[...]
    own_meta[17:18, 0:32] = pair_in[...]

    def normalize(i, carry):
        rows = pl.ds(pl.multiple_of(i * 128, 128), 128)
        values = emb[rows, :].astype(jnp.float32)
        scaled = values * lax.rsqrt(jnp.sum(values * values, axis=-1, keepdims=True) + 1e-06)
        unit = scaled.astype(jnp.bfloat16)
        for c in range(SLICES):
            own[c, i // 2, pl.ds(pl.multiple_of(lax.rem(i, 2) * 128, 128), 128), :] = unit[:, c * LANES:(c + 1) * LANES]
        return carry

    lax.fori_loop(0, 8, normalize, 0)
    pl.semaphore_wait(barrier, 31)

    started = []

    def remote(src, dst, send, recv, device):
        return pltpu.make_async_remote_copy(src_ref=src, dst_ref=dst, send_sem=send, recv_sem=recv, device_id=device,
                                            device_id_type=MESH)

    def go(copy):
        copy.start()
        started.append(copy)

    def queue_copy(k):
        kind, n = QUEUE[k]
        if kind == "o":
            c, src, dst = slice_id(phase, n), own, m1
        elif kind == "f":
            c, src, dst = slice_id(lax.rem(phase + 1, 4), n), m1, m2
        else:
            c, src, dst = slice_id(lax.rem(phase + 2, 4), n), m2, m3
        return remote(src.at[c], dst.at[c], q_send.at[k], q_recv.at[k], back)

    def queue_arrival(k):
        kind, n = QUEUE[k]
        if kind == "o":
            c, dst = slice_id(lax.rem(phase + 1, 4), n), m1
        elif kind == "f":
            c, dst = slice_id(lax.rem(phase + 2, 4), n), m2
        else:
            c, dst = slice_id(lax.rem(phase + 3, 4), n), m3
        return c, remote(dst.at[c], dst.at[c], q_send.at[k], q_recv.at[k], back)

    def forth_copy(i):
        c = slice_id(phase, i + 3)
        return remote(own.at[c], m3.at[c], fwd_send.at[i], fwd_recv.at[i], forth)

    def forth_arrival(i):
        c = slice_id(lax.rem(phase + 3, 4), i + 3)
        return c, remote(m3.at[c], m3.at[c], fwd_send.at[i], fwd_recv.at[i], forth)

    def side_copy(k):
        if k < 6:
            return remote(own.at[k], x1.at[k], e_send.at[k], e_recv.at[k], along)
        return remote(x1.at[k - 6], x2.at[k - 6], e_send.at[k], e_recv.at[k], along)

    def side_arrival(k):
        dst = x1.at[k] if k < 6 else x2.at[k - 6]
        return remote(dst, dst, e_send.at[k], e_recv.at[k], along)

    go(queue_copy(0))
    go(forth_copy(1))
    go(side_copy(0))
    go(queue_copy(1))
    go(forth_copy(2))
    go(side_copy(1))
    for i in range(9):
        go(remote(own_meta, metas[i], meta_send.at[i], meta_recv.at[i], at(holders[i])))
    go(remote(own, p0, d_send.at[0], d_recv.at[0], partner))

    shares = [0]

    def share(which, c):
        shares[0] += 1
        src, dst = bufs[which], bufs[which + P1]
        go(remote(src.at[c], dst.at[c], d_send.at[shares[0]], d_recv.at[which + 1], partner))

    def shared_arrival(i):
        dst = (p0, p1, p2, p3)[i]
        remote(dst, dst, d_send.at[0], d_recv.at[i], partner).wait_recv()

    def make_cols(meta, i):
        for part in range(2):
            for r in range(8):
                row = jnp.broadcast_to(meta[part * 8 + r:part * 8 + r + 1, :], (LANES, LANES))
                cols[2 * i + part][r // 2, (r % 2) * LANES:(r % 2 + 1) * LANES, :] = row.T

    def make_rows(meta, i):
        for part in range(2):
            for r in range(8):
                flats[i][r // 2, part:part + 1, (r % 2) * LANES:(r % 2 + 1) * LANES] = meta[part * 8 + r:part * 8 + r + 1, :]

    make_cols(own_meta, 0)
    make_rows(own_meta, 9)
    own_list = pltpu.make_async_copy(own_meta.at[pl.ds(16, 8)], lists[9], list_sem.at[9])
    own_list.start()
    for acc in accs:
        acc[...] = jnp.full((8, LANES), LOW, jnp.float32)
    row_ids = lax.broadcasted_iota(jnp.int32, (8, LANES), 0)

    def update(acc, block, row):
        spread = jnp.where(lax.rem(row_ids, 2) == 0, row[:, :LANES], row[:, LANES:])
        acc[...] = jnp.where(row_ids // 2 == block, jnp.maximum(acc[...], spread), acc[...])

    def tile(abuf, acol, aacc, a, bbuf, brows, bacc, b, same=False):
        left = jnp.concatenate([abuf[c, a] for c in range(SLICES)], axis=1)
        right = jnp.concatenate([bbuf[c, b] for c in range(SLICES)], axis=1)
        similar = lax.dot_general(left, right, (((1,), (1,)), ((), ())), preferred_element_type=jnp.float32)
        alab, arank = cols[2 * acol][a], cols[2 * acol + 1][a]
        brow = brows[b]
        for_a, for_b = None, []
        for h in range(2):
            blab = brow[0:1, h * LANES:(h + 1) * LANES]
            brank = brow[1:2, h * LANES:(h + 1) * LANES]
            value = jnp.where(alab == blab, similar[:, h * LANES:(h + 1) * LANES], LOW)
            later = brank < arank
            va = jnp.where(later, value, LOW)
            vb = jnp.where(arank < brank, value, LOW) if same else jnp.where(later, LOW, value)
            for_a = va if for_a is None else jnp.maximum(for_a, va)
            for_b.append(jnp.max(vb, axis=0, keepdims=True))
        update(aacc, a, jnp.max(for_a.T, axis=0, keepdims=True))
        update(bacc, b, jnp.concatenate(for_b, axis=1))

    def data(i):
        if i is None:
            return own, flats[9], lists[9], accs[9], me
        return bufs[i], flats[i], lists[i], accs[i], sources[i]

    def meet(ai, bi, forward=True, backward=True):
        abuf, _, alist, aacc, adev = data(ai)
        bbuf, brows, blist, bacc, bdev = data(bi)
        col = 0 if ai is None else ai + 1

        def one(i, carry):
            sends = i == 0
            a = jnp.where(sends, alist[0, bdev], alist[1, bdev])
            b = jnp.where(sends, blist[1, adev], blist[0, adev])
            tile(abuf, col, aacc, a, bbuf, brows, bacc, b)
            return carry

        lax.fori_loop(0 if forward else 1, 2 if backward else 1, one, 0)

    def local(lo, hi):
        def one(i, carry):
            k = jnp.where(i >= 4, 1, 0) + jnp.where(i >= 7, 1, 0) + jnp.where(i >= 9, 1, 0)
            l = i - pick(k, (0, 3, 5, 6))
            tile(own, 0, accs[9], k, own, flats[9], accs[9], l, same=True)
            return carry

        lax.fori_loop(lo, hi, one, 0)

    def have_meta(i):
        remote(metas[i], metas[i], meta_send.at[i], meta_recv.at[i], partner).wait_recv()
        copy = pltpu.make_async_copy(metas[i].at[pl.ds(16, 8)], lists[i], list_sem.at[i])
        copy.start()
        return copy

    def give_back(i):
        go(remote(accs[i], result_in.at[i], res_send.at[i], res_recv.at[i], at(sources[i])))

    local(0, 4)
    for k in range(15):
        c, copy = queue_arrival(k)
        copy.wait_recv()
        if k + 2 < 15:
            go(queue_copy(k + 2))
        share(ARRIVES[QUEUE[k][0]], c)
        if 2 <= k < 14:
            side_arrival(k - 2).wait_recv()
            if k < 12:
                go(side_copy(k))
        if k == 1:
            pending = [have_meta(i) for i in range(9)]
            for copy in pending:
                copy.wait()
            own_list.wait()
            for i in range(9):
                make_rows(metas[i], i)
            for i in range(3):
                make_cols(metas[i], i + 1)
        if k == 0:
            local(4, 10)
        if k == 2:
            shared_arrival(0)
            meet(None, P0, backward=False)
        if k == 3:
            for i in (1, 2):
                c, copy = forth_arrival(i)
                copy.wait_recv()
                share(M3, c)
        if k == 6:
            go(forth_copy(0))
        if k == 7:
            meet(None, X1)
        if k == 9:
            meet(None, M1)
            meet(M1, X1)
            meet(M1, P0, backward=False)
        if k == 10:
            shared_arrival(1)
            meet(None, P1, backward=False)
            meet(M1, P1, backward=False)
        if k == 11:
            meet(None, M2, forward=False)
            meet(M2, X1)
            meet(M2, P0, backward=False)
            meet(M2, P1, backward=False)
        if k == 12:
            shared_arrival(2)
            meet(None, P2, backward=False)
            meet(M1, P2, backward=False)
            meet(M2, P2, backward=False)
            c, copy = forth_arrival(0)
            copy.wait_recv()
            share(M3, c)
        if k == 13:
            meet(None, X2, forward=False)
            meet(M1, X2, forward=False)
            meet(M2, X2, forward=False)
            for i in (P0, P1):
                pass
    meet(M3, X2, forward=False)
    give_back(X2)
    meet(M3, X1)
    give_back(X1)
    meet(M3, P0, backward=False)
    give_back(P0)
    meet(M3, P1, backward=False)
    give_back(P1)
    meet(M3, P2, backward=False)
    give_back(P2)
    shared_arrival(3)
    meet(M3, P3, backward=False)
    give_back(M3)
    meet(M2, P3, backward=False)
    give_back(M2)
    meet(M1, P3, backward=False)
    give_back(M1)
    meet(None, P3, backward=False)
    give_back(P3)

    best = jnp.maximum(accs[9][...], 0.0)
    for i in range(9):
        remote(result_in.at[i], result_in.at[i], res_send.at[i], res_recv.at[i], partner).wait_recv()
        best = jnp.maximum(best, result_in[i])
    scores_out[...] = best
    for copy in started:
        copy.wait_send()


def exchange(embeddings, labels, ranking, send_list, pair_list):
    dataset = pltpu.VMEM((SLICES, 4, BLOCK, LANES), jnp.bfloat16)
    dma = pltpu.SemaphoreType.DMA
    return pl.pallas_call(
        kernel,
        out_shape=jax.ShapeDtypeStruct((8, LANES), jnp.float32),
        in_specs=[pl.BlockSpec(memory_space=pltpu.VMEM)] * 5,
        out_specs=pl.BlockSpec(memory_space=pltpu.VMEM),
        scratch_shapes=[dataset] * 10
        + [pltpu.VMEM((24, LANES), jnp.int32)] * 10
        + [pltpu.SMEM((8, LANES), jnp.int32)] * 10
        + [pltpu.VMEM((4, BLOCK, LANES), jnp.int32)] * 8
        + [pltpu.VMEM((8, LANES), jnp.float32)] * 10
        + [pltpu.VMEM((4, 8, BLOCK), jnp.int32)] * 10
        + [pltpu.VMEM((9, 8, LANES), jnp.float32),
           dma((15,)), dma((15,)), dma((3,)), dma((3,)), dma((12,)), dma((12,)), dma((20,)), dma((4,)),
           dma((9,)), dma((9,)), dma((10,)), dma((9,)), dma((9,))],
        compiler_params=pltpu.CompilerParams(collective_id=0, has_side_effects=True, vmem_limit_bytes=56 * 1024 * 1024),
    )(embeddings, labels.reshape(8, LANES), ranking.reshape(8, LANES), send_list, pair_list)


def body(embeddings, labels, ranking, send_list, pair_list):
    scores = exchange(embeddings, labels, ranking, send_list, pair_list).reshape(ROWS)
    values = embeddings.astype(jnp.float32)
    unit_rows = (values * lax.rsqrt(jnp.sum(values * values, axis=-1, keepdims=True) + 1e-06)).astype(jnp.bfloat16)
    cluster_ids = jnp.arange(K, dtype=jnp.int32)
    indicator = (cluster_ids[:, None] == labels[None, :]).astype(jnp.bfloat16)
    totals = lax.psum_scatter(
        jnp.dot(indicator, unit_rows, preferred_element_type=jnp.float32),
        ("group", "dev"),
        scatter_dimension=0,
        tiled=True,
    )
    centroids = totals * lax.rsqrt(jnp.mean(totals * totals, axis=-1, keepdims=True) + 1e-06)
    return (scores, centroids)


def solution(mesh):
    return jax.shard_map(
        body,
        mesh=mesh,
        in_specs=(
            P(("group", "dev"), None),
            P(("group", "dev")),
            P(("group", "dev")),
            P(("group", "dev"), None),
            P(("group", "dev"), None),
        ),
        out_specs=(P(("group", "dev")), P(("group", "dev"), None)),
        check_vma=False,
    )
```

time: 305 us -> 257 us (0.84)
  Pallas kernels: 0 us -> 70 us
  starting transfers between devices: 43.1 us -> 0.04 us
  waiting for transfers between devices: 190 us -> 155 us
  local copies, waits for them, and re-layouts: 20.2 us -> 1.27 us
  matrix products: 25.1 us -> 11.7 us
  loops' own time: 3.93 us -> 0 us
    all_to_all x4 -> x0, waiting for transfers between devices: 190 us -> none  [the longest x1 176 us: body(): lax.all_to_all(outgoing[0], 'dev', split_axis=0, concat_axis=0, tiled=True)]
    reduce_scatter x1, waiting for transfers between devices: 0.01 us -> 155 us  [body(): lax.psum_scatter(jnp.dot(indicator, unit_rows, preferred_element_type=jnp...]
    pallas_call x0 -> x1, Pallas kernels: none -> 70 us  [exchange(): pl.pallas_call(kernel, out_shape=jax.ShapeDtypeStruct((8, LANES), jnp.flo...]
    all_to_all x4 -> x0, starting transfers between devices: 43.1 us -> none  [the longest x1 24.1 us: body(): lax.all_to_all(for_arrived, 'dev', split_axis=0, concat_axis=0, tiled=True)]
    gather x6 -> x0, local copies, waits for them, and re-layouts: 16 us -> none  [the longest x3 8.01 us: body(): outgoing = (blocks[sent_ids], block_labels[sent_ids], block_ranks[sent_ids])]
    dot_general x3 -> x0, matrix products: 13.6 us -> none  [the longest x1 11.3 us: body(): jnp.einsum('pjd,pid->pji', arrived, mine_rows, preferred_element_type=jnp...]
    another operation x1 -> x0, loops' own time: 3.93 us -> none  [body(): local_scores = lax.map(local_part, starts).reshape(point_count)]
  transfers between devices with their start and end apart: 5 -> 1, of which waited for: 4 -> 1; matrix products, arithmetic and copies ran while one was open for 11% -> 0% of each run, Pallas kernels for 0% -> 27%
where the time goes in v1:
time: 257 us; the launch traced here: 256 us
  waiting for transfers between devices  155 us (60%)
  Pallas kernels  70 us (27%)
  between operations  14 us (5%)
  matrix products  11.7 us (5%)
  other arithmetic  4.42 us (2%)
    reduce_scatter x1, waiting for transfers between devices, body(): lax.psum_scatter(jnp.dot(indicator, unit_rows, preferred_element_type=jnp...  155 us
    pallas_call x1, Pallas kernels, exchange(): pl.pallas_call(kernel, out_shape=jax.ShapeDtypeStruct((8, LANES), jnp.flo...  70 us
    dot_general x1, matrix products, body(): jnp.dot(indicator, unit_rows, preferred_element_type=jnp.float32)  11.7 us
  transfers between devices with their start and end apart: 1, of which 1 were waited for; matrix products, arithmetic and copies ran while one was open for 0% of the time, Pallas kernels for 27%

profile of v1, /device:TPU:0, one launch (start us, length us, event | category | flops | bytes accessed | tf_op | source)
XLA Modules:
  0.0 256.3 jit_solution(4092665599227668817)
XLA Ops:
  7.2 0.0 reduce-scatter.2.cloned.1.call-start
  7.2 1.8 fusion.2
  9.0 11.7 %fusion = f32[4096,768]{1,0:T(8,128)} fusion(s32[1024]{0:T(1024)} %param.6, bf16[1024,768]{1,0:T(8,128)(2,1)} %emb.1, f32[1024]{0:T(1024)S(1)} %add_rsqrt_fusion), kind=kOutput, calls=%fused_computation.1 | convolution fusion | flops 6449004544 | bytes 14163968 | tf_op jit(solution)/shard_map/dot_general | solution.py:360
  20.7 0.0 reduce-scatter.2.cloned.1.call-update
  20.7 70.0 %shard_map.68 = f32[8,128]{1,0:T(8,128)} custom-call(bf16[1024,768]{1,0:T(8,128)(2,1)} %emb.1, s32[8,128]{1,0:T(8,128)} %bitcast.4, s32[8,128]{1,0:T(8,128)} %bitcast.5, s32[1,32]{1,0:T(1,128)} %send_in.1, s32[1,32]{1,0:T(1,128)} %pair_in.1), custom_call_target="tpu_custom_call" | custom-call | tf_op jit(solution)/shard_map/pallas_call | solution.py:335
  90.7 154.8 %reduce-scatter.2.cloned.1.call-done = f32[32,768]{1,0:T(8,128)} async-done(((f32[4096,768]{1,0:T(8,128)}), f32[32,768]{1,0:T(8,128)}) %reduce-scatter.2.cloned.1.call-update) | async-done | bytes 98320 | tf_op jit(solution)/shard_map/reduce_scatter | solution.py:359
  245.6 1.0 multiply_reduce_fusion
  246.6 1.6 broadcast_multiply_fusion
  248.2 1.3 copy.8
  (2 shorter events, 0.0 us)
Async XLA Ops:
  7.2 238.4 %reduce-scatter.2.cloned.1.call-start = ((), (), s32[]{:S(2)}) async-start(), calls=%async_computation.1 | async-start | bytes 12681216 | tf_op jit(solution)/shard_map/reduce_scatter | solution.py:359
Sparse Core Ops, SparseCore 0:
  20.8 224.7 reduce-scatter.1

commit v2 on v1

v2 whole, which is shorter than its diff:
```python
import jax
import jax.numpy as jnp
from jax import lax
from jax.experimental import pallas as pl
from jax.experimental.pallas import tpu as pltpu
from jax.sharding import PartitionSpec as P

K = 4096
BLOCK = 256
ROWS = 1024
SLICES = 6
LANES = 128
LOW = -2.0
MESH = pl.DeviceIdType.MESH
WINDOW = 4
M1, M2, M3, X1, X2, P0, P1, P2, P3 = range(9)
QUEUE = ([("o", n) for n in range(6)] + [("f", n) for n in range(6)] + [("g", n) for n in range(3)])


def kernel(emb, lab_in, rank_in, send_in, pair_in, scores_out, centroids_out,
           own, m1, m2, m3, x1, x2, p0, p1, p2, p3, *rest):
    metas = rest[0:10]
    lists = rest[10:20]
    cols = rest[20:28]
    accs = rest[28:38]
    flats = rest[38:48]
    own_meta = metas[9]
    (result_in, halves, xa, xp, xmeta, rhs, ids_row, ids_side, sums, cores, from_core, in_f, in_b, in2_f, in2_b, in_side, in_x,
     q_send, q_recv, fwd_send, fwd_recv, e_send, e_recv, d_send, d_recv, meta_send, meta_recv, list_sem, res_send, res_recv,
     x_send, x_recv, c_send, c_recv) = rest[48:]
    bufs = (m1, m2, m3, x1, x2, p0, p1, p2, p3)
    group = lax.axis_index("group")
    me = lax.axis_index("dev")
    core = lax.rem(me, 2)
    y, z = me // 8, lax.rem(me // 2, 4)
    main = jnp.where(core == 0, z, y)
    side = jnp.where(core == 0, y, z)
    def place(u, w, e):
        return lax.rem(u, 4) * (2 + 6 * e) + lax.rem(w, 4) * (8 - 6 * e) + e

    def at(index):
        return (group, index)

    other = 1 - core
    sources = [place(main + 1, side, core), place(main + 2, side, core), place(main + 3, side, core),
               place(main, side + 3, core), place(main, side + 2, core),
               place(side, main, other), place(side + 1, main, other), place(side + 2, main, other), place(side + 3, main, other)]
    back = at(place(main + 3, side, core))
    forth = at(place(main + 1, side, core))
    along = at(place(main, side + 1, core))
    partner = at(place(side, main, other))

    behind = at(place(main, side + 3, core))
    across = at(place(main, side + 2, core))
    mates = [(lax.rem(group + i, 4), me) for i in (1, 2, 3)]

    barrier = pltpu.get_barrier_semaphore()
    for device in [forth, back, along, behind, partner] + mates:
        pl.semaphore_signal(barrier, inc=1, device_id=device, device_id_type=MESH)

    own_meta[0:8, :] = lab_in[...]
    own_meta[8:16, :] = rank_in[...]
    own_meta[16:17, 0:32] = send_in[...]
    own_meta[17:18, 0:32] = pair_in[...]

    def normalize(i, carry):
        rows = pl.ds(pl.multiple_of(i * 128, 128), 128)
        values = emb[rows, :].astype(jnp.float32)
        scaled = values * lax.rsqrt(jnp.sum(values * values, axis=-1, keepdims=True) + 1e-06)
        unit = scaled.astype(jnp.bfloat16)
        for c in range(SLICES):
            own[c, i // 2, pl.ds(pl.multiple_of(lax.rem(i, 2) * 128, 128), 128), :] = unit[:, c * LANES:(c + 1) * LANES]
        return carry

    lax.fori_loop(0, 8, normalize, 0)
    lane_ids = lax.broadcasted_iota(jnp.int32, (BLOCK, LANES), 1)

    for t in range(2):
        for b in range(2):
            low = own[4 + t, b].astype(jnp.float32)
            high = own[4 + t, b + 2].astype(jnp.float32)
            halves[2 * t, b] = jnp.where(lane_ids < 64, low, pltpu.roll(high, 64, 1)).astype(jnp.bfloat16)
            halves[2 * t + 1, b] = jnp.where(lane_ids < 64, pltpu.roll(low, 64, 1), high).astype(jnp.bfloat16)
    pl.semaphore_wait(barrier, 8)

    started = []

    def remote(src, dst, send, recv, device):
        return pltpu.make_async_remote_copy(src_ref=src, dst_ref=dst, send_sem=send, recv_sem=recv, device_id=device,
                                            device_id_type=MESH)

    def go(copy):
        copy.start()
        started.append(copy)

    rings = {"o": (own, m1), "f": (m1, m2), "g": (m2, m3)}

    def queue_copy(k):
        kind, n = QUEUE[k]
        src, dst = rings[kind]
        return remote(src.at[n], dst.at[n], q_send.at[k], q_recv.at[k], back)

    def forth_copy(i):
        return remote(own.at[i + 3], m3.at[i + 3], fwd_send.at[i], fwd_recv.at[i], forth)

    def side_copy(k):
        if k < 6:
            return remote(own.at[k], x1.at[k], e_send.at[k], e_recv.at[k], along)
        return remote(x1.at[k - 6], x2.at[k - 6], e_send.at[k], e_recv.at[k], along)

    def side_arrival(k):
        dst = x1.at[k] if k < 6 else x2.at[k - 6]
        return remote(dst, dst, e_send.at[k], e_recv.at[k], along)

    meta_routes = [(9, M1, back), (9, M3, forth), (9, X1, along), (9, P0, partner),
                   (M1, M2, back), (X1, X2, along), (M1, P1, partner), (M3, P3, partner), (M2, P2, partner)]

    def meta_go(i):
        src, dst, device = meta_routes[i]
        go(remote(metas[src], metas[dst], meta_send.at[i], meta_recv.at[dst], device))

    def mate_copies(i):
        quarter = lax.rem(group + 1 + i, 4)
        go(remote(own_meta.at[pl.ds(0, 8)], xmeta.at[i], x_send.at[i, 0], x_recv.at[i, 0], mates[i]))
        go(remote(own.at[quarter], xa.at[i], x_send.at[i, 1], x_recv.at[i, 1], mates[i]))
        go(remote(halves.at[quarter], xp.at[i], x_send.at[i, 2], x_recv.at[i, 2], mates[i]))

    go(queue_copy(0))
    go(side_copy(0))
    mate_copies(0)
    mate_copies(2)
    for i in range(4):
        meta_go(i)
    go(queue_copy(1))
    go(side_copy(1))
    go(remote(own, p0, d_send.at[0], d_recv.at[0], partner))
    mate_copies(1)
    for k in range(2, WINDOW):
        go(queue_copy(k))
        go(side_copy(k))

    def share(which, first, count, slot):
        src, dst = bufs[which], bufs[which + P1]
        go(remote(src.at[pl.ds(first, count)], dst.at[pl.ds(first, count)], d_send.at[slot], d_recv.at[which + 1], partner))

    def shared_arrival(i):
        dst = (p0, p1, p2, p3)[i]
        remote(dst, dst, d_send.at[0], d_recv.at[i], partner).wait_recv()

    def landed(dst, recv):
        remote(dst, dst, res_send.at[0], recv, partner).wait_recv()

    def make_cols(meta, i):
        for part in range(2):
            for r in range(8):
                row = jnp.broadcast_to(meta[part * 8 + r:part * 8 + r + 1, :], (LANES, LANES))
                cols[2 * i + part][r // 2, (r % 2) * LANES:(r % 2 + 1) * LANES, :] = row.T

    def make_rows(meta, i):
        for part in range(2):
            for r in range(8):
                flats[i][r // 2, part:part + 1, (r % 2) * LANES:(r % 2 + 1) * LANES] = meta[part * 8 + r:part * 8 + r + 1, :]

    make_cols(own_meta, 0)
    make_rows(own_meta, 9)
    own_list = pltpu.make_async_copy(own_meta.at[pl.ds(16, 8)], lists[9], list_sem.at[9])
    own_list.start()
    for acc in accs:
        acc[...] = jnp.full((8, LANES), LOW, jnp.float32)
    row_ids = lax.broadcasted_iota(jnp.int32, (8, LANES), 0)

    def update(acc, block, row):
        spread = jnp.where(lax.rem(row_ids, 2) == 0, row[:, :LANES], row[:, LANES:])
        acc[...] = jnp.where(row_ids // 2 == block, jnp.maximum(acc[...], spread), acc[...])

    def tile(abuf, acol, aacc, a, bbuf, brows, bacc, b, same=False):
        left = jnp.concatenate([abuf[c, a] for c in range(SLICES)], axis=1)
        right = jnp.concatenate([bbuf[c, b] for c in range(SLICES)], axis=1)
        similar = lax.dot_general(left, right, (((1,), (1,)), ((), ())), preferred_element_type=jnp.float32)
        alab, arank = cols[2 * acol][a], cols[2 * acol + 1][a]
        brow = brows[b]
        for_a, for_b = None, []
        for h in range(2):
            blab = brow[0:1, h * LANES:(h + 1) * LANES]
            brank = brow[1:2, h * LANES:(h + 1) * LANES]
            value = jnp.where(alab == blab, similar[:, h * LANES:(h + 1) * LANES], LOW)
            later = brank < arank
            va = jnp.where(later, value, LOW)
            vb = jnp.where(arank < brank, value, LOW) if same else jnp.where(later, LOW, value)
            for_a = va if for_a is None else jnp.maximum(for_a, va)
            for_b.append(jnp.max(vb, axis=0, keepdims=True))
        update(aacc, a, jnp.max(for_a.T, axis=0, keepdims=True))
        update(bacc, b, jnp.concatenate(for_b, axis=1))

    def data(i):
        if i is None:
            return own, flats[9], lists[9], accs[9], me
        return bufs[i], flats[i], lists[i], accs[i], sources[i]

    def meet(ai, bi, forward=True, backward=True):
        abuf, _, alist, aacc, adev = data(ai)
        bbuf, brows, blist, bacc, bdev = data(bi)
        col = 0 if ai is None else ai + 1

        def one(i, carry):
            sends = i == 0
            a = jnp.where(sends, alist[0, bdev], alist[1, bdev])
            b = jnp.where(sends, blist[1, adev], blist[0, adev])
            tile(abuf, col, aacc, a, bbuf, brows, bacc, b)
            return carry

        lax.fori_loop(0 if forward else 1, 2 if backward else 1, one, 0)

    def local(lo, hi):
        def one(i, carry):
            k = jnp.where(i >= 4, 1, 0) + jnp.where(i >= 7, 1, 0) + jnp.where(i >= 9, 1, 0)
            l = i - 3 * jnp.where(i >= 4, 1, 0) - 2 * jnp.where(i >= 7, 1, 0) - jnp.where(i >= 9, 1, 0)
            tile(own, 0, accs[9], k, own, flats[9], accs[9], l, same=True)
            return carry

        lax.fori_loop(lo, hi, one, 0)

    def have_meta(i):
        landed(metas[i], meta_recv.at[i])

    def use_meta(i):
        copy = pltpu.make_async_copy(metas[i].at[pl.ds(16, 8)], lists[i], list_sem.at[i])
        copy.start()
        make_rows(metas[i], i)
        if i < 3:
            make_cols(metas[i], i + 1)
        copy.wait()

    rows_iota = lax.broadcasted_iota(jnp.int32, (BLOCK, LANES), 0)
    ids_row[...] = lax.rem(rows_iota // 32, 4) * 1024 + lax.rem(rows_iota, 32)
    ids_side[...] = rows_iota // 128

    def set_source(points, extra):
        for b in range(4):
            rhs[b * BLOCK:(b + 1) * BLOCK, :LANES] = points[b]
            keep = (lane_ids < 64) if b < 2 else (lane_ids >= 64)
            rhs[b * BLOCK:(b + 1) * BLOCK, LANES:] = jnp.where(keep, extra[b % 2].astype(jnp.float32), 0.0).astype(jnp.bfloat16)

    def add_source(labels, lo, hi, mode):
        def chunk(i, carry):
            m = lax.rem(i + 8 * other, 16)
            e1, m1_, h = m // 8, lax.rem(m // 2, 4), lax.rem(m, 2)
            step = 256 - 192 * e1
            base = e1 * 32 + m1_ * (64 + 192 * e1) + 2 * h * step
            ids = ids_row[...] + ids_side[...] * step + base
            hot = jnp.concatenate(
                [jnp.where(labels[r:r + 1, :] == ids, 1.0, 0.0).astype(jnp.bfloat16) for r in range(8)], axis=1)
            total = jnp.dot(hot, rhs[...], preferred_element_type=jnp.float32)
            if mode != "first":
                total = total + sums[m]
            if mode != "last":
                sums[m] = total
            else:
                extra = total[:, LANES:]
                extra = extra + pltpu.roll(extra, 64, 1)
                for b in range(8):
                    rows = slice(b * 32, b * 32 + 32)
                    cores[e1, m1_, 2 * h + b // 4, b % 4, 0:32, :] = total[rows, :LANES]
                    cores[e1, m1_, 2 * h + b // 4, b % 4, 32:48, :] = jnp.where(
                        lane_ids[:16] < 64, extra[b * 32:b * 32 + 16], extra[b * 32 + 16:b * 32 + 32])
            return carry

        lax.fori_loop(lo, hi, chunk, 0)

    def ring(i):
        return lax.rem(main + i, 4)

    def centroid_send(src, dst, i, device):
        go(remote(src, dst, c_send.at[i], c_recv.at[i], device))

    def finish_centroids():
        quarters = [in_x[lax.rem(group - q + 4, 4)] for q in range(4)]
        tiles = [quarters[q][0:32] for q in range(4)]
        low = lane_ids[:16] < 64
        for t in range(2):
            even, odd = quarters[2 * t][32:48], quarters[2 * t + 1][32:48]
            tiles.append(jnp.concatenate([jnp.where(low, even, pltpu.roll(odd, 64, 1)),
                                          jnp.where(low, pltpu.roll(even, 64, 1), odd)], axis=0))
        squares = tiles[0] * tiles[0]
        for tile_values in tiles[1:]:
            squares = squares + tile_values * tile_values
        scale = lax.rsqrt(jnp.sum(squares, axis=-1, keepdims=True) / 768.0 + 1e-06)
        for c in range(SLICES):
            centroids_out[:, c * LANES:(c + 1) * LANES] = tiles[c] * scale

    def give_back(i):
        go(remote(accs[i], result_in.at[i], res_send.at[i], res_recv.at[i], at(sources[i])))

    def source(i):
        landed(xmeta.at[i], x_recv.at[i, 0])
        landed(xa.at[i], x_recv.at[i, 1])
        landed(xp.at[i], x_recv.at[i, 2])
        set_source(xa.at[i], xp.at[i])

    own_list.wait()
    local(0, 3)
    for k in range(15):
        kind, n = QUEUE[k]
        landed(rings[kind][1].at[n], q_recv.at[k])
        if k + WINDOW < 15:
            go(queue_copy(k + WINDOW))
        if 2 <= k < 14:
            dst = x1.at[k - 2] if k < 8 else x2.at[k - 8]
            landed(dst, e_recv.at[k - 2])
            if k - 2 + WINDOW < 12:
                go(side_copy(k - 2 + WINDOW))
        if k == 0:
            have_meta(M1)
            meta_go(4)
            meta_go(6)
            have_meta(X1)
            meta_go(5)
            have_meta(M3)
            meta_go(7)
            have_meta(P0)
            local(3, 6)
        if k == 1:
            have_meta(M2)
            meta_go(8)
            for i in (M1, M3, X1, P0, M2):
                use_meta(i)
            local(6, 10)
        if k == 2:
            for i in (X2, P1, P2, P3):
                have_meta(i)
                use_meta(i)
            set_source(own.at[group], halves.at[group])
            add_source(own_meta, 0, 8, "first")
        if k == 3:
            add_source(own_meta, 8, 16, "first")
        if 3 <= k < 6:
            go(forth_copy(k - 3))
        if k == 4:
            shared_arrival(0)
            meet(None, P0, backward=False)
        if k == 5:
            share(M1, 0, 6, 1)
            meet(None, M1)
            meet(M1, P0, backward=False)
        if k == 6:
            source(0)
            add_source(xmeta.at[0], 0, 16, "add")
        if k == 7:
            source(2)
            add_source(xmeta.at[2], 0, 16, "add")
        if k == 8:
            source(1)
            add_source(xmeta.at[1], 0, 8, "last")
            centroid_send(cores.at[other], from_core, 0, partner)
            add_source(xmeta.at[1], 8, 16, "last")
        if k == 9:
            meet(None, X1)
            meet(M1, X1)
            landed(from_core, c_recv.at[0])
            for i in range(4):
                cores[core, i] = cores[core, i] + from_core[i]
            centroid_send(cores.at[core, ring(2), pl.ds(0, 2)], in_f, 1, forth)
            centroid_send(cores.at[core, ring(2), pl.ds(2, 2)], in_b, 2, back)
        if k == 10:
            shared_arrival(1)
            meet(None, P1, backward=False)
            meet(M1, P1, backward=False)
            landed(in_f, c_recv.at[1])
            cores[core, ring(1), 0:2] = cores[core, ring(1), 0:2] + in_f[...]
            centroid_send(cores.at[core, ring(1)], in2_f, 3, forth)
            landed(in_b, c_recv.at[2])
            cores[core, ring(3), 2:4] = cores[core, ring(3), 2:4] + in_b[...]
            centroid_send(cores.at[core, ring(3)], in2_b, 4, back)
        if k == 11:
            share(M2, 0, 6, 2)
            meet(None, M2, forward=False)
            meet(M2, X1)
            meet(M2, P0, backward=False)
            meet(M2, P1, backward=False)
        if k == 12:
            for i in range(3):
                landed(m3.at[i + 3], fwd_recv.at[i])
            share(M3, 3, 3, 3)
            landed(in2_f, c_recv.at[3])
            landed(in2_b, c_recv.at[4])
            cores[core, main] = cores[core, main] + in2_f[...] + in2_b[...]
            for i, device in ((1, along), (2, across), (3, behind)):
                centroid_send(cores.at[core, main, lax.rem(side + i, 4)], in_side.at[i], 4 + i, device)
            shared_arrival(2)
            meet(None, P2, backward=False)
            meet(M1, P2, backward=False)
            meet(M2, P2, backward=False)
        if k == 13:
            share(M3, 0, 2, 4)
            meet(None, X2, forward=False)
            meet(M1, X2, forward=False)
            meet(M2, X2, forward=False)
    share(M3, 2, 1, 5)
    for i in (1, 2, 3):
        landed(in_side.at[i], c_recv.at[4 + i])
    in_side[0] = cores[core, main, side] + in_side[1] + in_side[2] + in_side[3]
    in_x[0] = in_side[0, group]
    for i in (1, 2, 3):
        centroid_send(in_side.at[0, lax.rem(group + i, 4)], in_x.at[i], 7 + i, mates[i - 1])
    meet(M3, X2, forward=False)
    give_back(X2)
    meet(M3, X1)
    give_back(X1)
    meet(M3, P0, backward=False)
    give_back(P0)
    meet(M3, P1, backward=False)
    give_back(P1)
    meet(M3, P2, backward=False)
    give_back(P2)
    shared_arrival(3)
    meet(M3, P3, backward=False)
    give_back(M3)
    meet(M2, P3, backward=False)
    give_back(M2)
    meet(M1, P3, backward=False)
    give_back(M1)
    meet(None, P3, backward=False)
    give_back(P3)

    for i in (1, 2, 3):
        landed(in_x.at[i], c_recv.at[7 + i])
    finish_centroids()
    best = jnp.maximum(accs[9][...], 0.0)
    for i in range(9):
        remote(result_in.at[i], result_in.at[i], res_send.at[i], res_recv.at[i], partner).wait_recv()
        best = jnp.maximum(best, result_in[i])
    scores_out[...] = best
    for copy in started:
        copy.wait_send()


def exchange(embeddings, labels, ranking, send_list, pair_list):
    dataset = pltpu.VMEM((SLICES, 4, BLOCK, LANES), jnp.bfloat16)
    dma = pltpu.SemaphoreType.DMA
    f32, bf16, i32 = jnp.float32, jnp.bfloat16, jnp.int32
    return pl.pallas_call(
        kernel,
        out_shape=(jax.ShapeDtypeStruct((8, LANES), f32), jax.ShapeDtypeStruct((32, SLICES * LANES), f32)),
        in_specs=[pl.BlockSpec(memory_space=pltpu.VMEM)] * 5,
        out_specs=(pl.BlockSpec(memory_space=pltpu.VMEM), pl.BlockSpec(memory_space=pltpu.VMEM)),
        scratch_shapes=[dataset] * 10
        + [pltpu.VMEM((24, LANES), i32)] * 10
        + [pltpu.SMEM((8, LANES), i32)] * 10
        + [pltpu.VMEM((4, BLOCK, LANES), i32)] * 8
        + [pltpu.VMEM((8, LANES), f32)] * 10
        + [pltpu.VMEM((4, 8, BLOCK), i32)] * 10
        + [pltpu.VMEM((9, 8, LANES), f32),
           pltpu.VMEM((4, 2, BLOCK, LANES), bf16),
           pltpu.VMEM((3, 4, BLOCK, LANES), bf16),
           pltpu.VMEM((3, 2, BLOCK, LANES), bf16),
           pltpu.VMEM((3, 8, LANES), i32),
           pltpu.VMEM((ROWS, 2 * LANES), bf16),
           pltpu.VMEM((BLOCK, LANES), i32),
           pltpu.VMEM((BLOCK, LANES), i32),
           pltpu.VMEM((16, BLOCK, 2 * LANES), f32),
           pltpu.VMEM((2, 4, 4, 4, 48, LANES), f32),
           pltpu.VMEM((4, 4, 4, 48, LANES), f32),
           pltpu.VMEM((2, 4, 48, LANES), f32),
           pltpu.VMEM((2, 4, 48, LANES), f32),
           pltpu.VMEM((4, 4, 48, LANES), f32),
           pltpu.VMEM((4, 4, 48, LANES), f32),
           pltpu.VMEM((4, 4, 48, LANES), f32),
           pltpu.VMEM((4, 48, LANES), f32),
           dma((15,)), dma((15,)), dma((3,)), dma((3,)), dma((12,)), dma((12,)), dma((6,)), dma((4,)),
           dma((9,)), dma((9,)), dma((10,)), dma((9,)), dma((9,)), dma((3, 3)), dma((3, 3)), dma((11,)), dma((11,))],
        compiler_params=pltpu.CompilerParams(collective_id=0, has_side_effects=True, vmem_limit_bytes=60 * 1024 * 1024),
    )(embeddings, labels.reshape(8, LANES), ranking.reshape(8, LANES), send_list, pair_list)


def body(embeddings, labels, ranking, send_list, pair_list):
    scores, centroids = exchange(embeddings, labels, ranking, send_list, pair_list)
    return (scores.reshape(ROWS), centroids)


def solution(mesh):
    return jax.shard_map(
        body,
        mesh=mesh,
        in_specs=(
            P(("group", "dev"), None),
            P(("group", "dev")),
            P(("group", "dev")),
            P(("group", "dev"), None),
            P(("group", "dev"), None),
        ),
        out_specs=(P(("group", "dev")), P(("group", "dev"), None)),
        check_vma=False,
    )
```

time: 257 us -> 94 us (0.37)
  waiting for transfers between devices: 155 us -> 0 us
  Pallas kernels: 70 us -> 88.8 us
  between operations: 14 us -> 0.64 us
  matrix products: 11.7 us -> 0 us
  other arithmetic: 4.42 us -> 0 us
    reduce_scatter x1 -> x0, waiting for transfers between devices: 155 us -> none  [body(): lax.psum_scatter(jnp.dot(indicator, unit_rows, preferred_element_type=jnp...]
    pallas_call x1, Pallas kernels: 70 us -> 88.8 us  [exchange(): pl.pallas_call(kernel, out_shape=(jax.ShapeDtypeStruct((8, LANES), f32),...]
    dot_general x1 -> x0, matrix products: 11.7 us -> none  [body(): jnp.dot(indicator, unit_rows, preferred_element_type=jnp.float32)]
    reduce_sum x2 -> x0, other arithmetic: 2.79 us -> none  [the longest x1 1.78 us: body(): jnp.sum(values * values, axis=-1, keepdims=True) + 1e-06]
  transfers between devices with their start and end apart: 1 -> 0, of which waited for: 1 -> 0; matrix products, arithmetic and copies ran while one was open for 0% -> 0% of each run, Pallas kernels for 27% -> 0%
where the time goes in v2:
time: 94 us; the launch traced here: 92.2 us
  Pallas kernels  88.8 us (94%)
  local copies, waits for them, and re-layouts  2.81 us (3%)
    pallas_call x1, Pallas kernels, exchange(): pl.pallas_call(kernel, out_shape=(jax.ShapeDtypeStruct((8, LANES), f32),...  88.8 us
    unnamed x2, local copies, waits for them, and re-layouts  2.81 us

profile of v2, /device:TPU:0, one launch (start us, length us, event | category | flops | bytes accessed | tf_op | source)
XLA Modules:
  0.0 92.2 jit_solution(13069154941145862731)
XLA Ops:
  0.6 88.8 %shard_map.68 = (f32[8,128]{1,0:T(8,128)}, f32[32,768]{1,0:T(8,128)}) custom-call(bf16[1024,768]{1,0:T(8,128)(2,1)} %emb.1, s32[8,128]{1,0:T(8,128)} %bitcast.3, s32[8,128]{1,0:T(8,128)} %bitcast.4, s32[1,32]{1,0:T(1,128)} %send_in.1, s32[1,32]{1,0:T(1,128)} %pair_in.1), custom_call_target="tpu_custom_call" | custom-call | tf_op jit(solution)/shard_map/pallas_call | solution.py:441
  89.4 1.3 %copy.9 = f32[1024]{0:T(1024)} copy(f32[1024]{0:T(1024)} %bitcast.5) | data formatting | bytes 8192
  90.7 1.5 %copy.10 = f32[32,768]{1,0:T(8,128)} copy(f32[32,768]{1,0:T(8,128)} %get-tuple-element.9) | data formatting | bytes 196608

commit v3 on v2

v3 whole, which is shorter than its diff:
```python
import jax
import jax.numpy as jnp
from jax import lax
from jax.experimental import pallas as pl
from jax.experimental.pallas import tpu as pltpu
from jax.sharding import PartitionSpec as P

K = 4096
BLOCK = 256
ROWS = 1024
SLICES = 6
LANES = 128
LOW = -2.0
RANKS = 131072
MESH = pl.DeviceIdType.MESH
M1, M2, M3, X1, X2, P0, P1, P2, P3 = range(9)
PARTS = ((0, 1), (1, 2), (3, 3))


def kernel(emb_in, lab_in, rank_in, send_in, pair_in, scores_out, centroids_out,
           own, m1, m2, m3, x1, x2, p0, p1, p2, p3, *rest):
    metas = rest[0:11]
    lists = rest[11:21]
    cols = rest[21:25]
    accs = rest[25:35]
    flats = rest[35:45]
    own_meta = metas[9]
    (result_in, halves, xa, xp, xmeta, rhs, sums, cores, from_core, in_f, in_b, in2_f, in2_b, in_side, in_x,
     q_send, q_recv, d_send, d_recv, meta_send, meta_recv, list_sem, res_send, res_recv,
     x_send, x_recv, c_send, c_recv, emb, emb_sem) = rest[45:]
    bufs = (m1, m2, m3, x1, x2, p0, p1, p2, p3)
    group = lax.axis_index("group")
    me = lax.axis_index("dev")
    core = lax.rem(me, 2)
    y, z = me // 8, lax.rem(me // 2, 4)
    main = jnp.where(core == 0, z, y)
    side = jnp.where(core == 0, y, z)
    def place(u, w, e):
        return lax.rem(u, 4) * (2 + 6 * e) + lax.rem(w, 4) * (8 - 6 * e) + e

    def at(index):
        return (group, index)

    other = 1 - core
    sources = [place(main + 1, side, core), place(main + 2, side, core), place(main + 3, side, core),
               place(main, side + 3, core), place(main, side + 2, core),
               place(side, main, other), place(side + 1, main, other), place(side + 2, main, other), place(side + 3, main, other)]
    back = at(place(main + 3, side, core))
    forth = at(place(main + 1, side, core))
    along = at(place(main, side + 1, core))
    partner = at(place(side, main, other))

    behind = at(place(main, side + 3, core))
    across = at(place(main, side + 2, core))
    mates = [(lax.rem(group + i, 4), me) for i in (1, 2, 3)]

    barrier = pltpu.get_barrier_semaphore()
    for device in [forth, back, along, behind, partner] + mates:
        pl.semaphore_signal(barrier, inc=1, device_id=device, device_id_type=MESH)

    emb_copy = pltpu.make_async_copy(emb_in, emb, emb_sem.at[0])
    emb_copy.start()
    own_meta[0:8, :] = lab_in[...] * RANKS + rank_in[...]
    own_meta[8:9, 0:32] = send_in[...]
    own_meta[9:10, 0:32] = pair_in[...]

    def normalize(i, carry):
        rows = pl.ds(pl.multiple_of(i * 128, 128), 128)
        values = emb[rows, :].astype(jnp.float32)
        scaled = values * lax.rsqrt(jnp.sum(values * values, axis=-1, keepdims=True) + 1e-06)
        unit = scaled.astype(jnp.bfloat16)
        for c in range(SLICES):
            own[c, i // 2, pl.ds(pl.multiple_of(lax.rem(i, 2) * 128, 128), 128), :] = unit[:, c * LANES:(c + 1) * LANES]
        return carry

    emb_copy.wait()
    lax.fori_loop(0, 8, normalize, 0)
    lane_ids = lax.broadcasted_iota(jnp.int32, (BLOCK, LANES), 1)

    for t in range(2):
        for b in range(2):
            low = own[4 + t, b].astype(jnp.float32)
            high = own[4 + t, b + 2].astype(jnp.float32)
            halves[2 * t, b] = jnp.where(lane_ids < 64, low, pltpu.roll(high, 64, 1)).astype(jnp.bfloat16)
            halves[2 * t + 1, b] = jnp.where(lane_ids < 64, pltpu.roll(low, 64, 1), high).astype(jnp.bfloat16)
    pl.semaphore_wait(barrier, 8)

    started = []

    def remote(src, dst, send, recv, device):
        return pltpu.make_async_remote_copy(src_ref=src, dst_ref=dst, send_sem=send, recv_sem=recv, device_id=device,
                                            device_id_type=MESH)

    def go(copy):
        copy.start()
        started.append(copy)

    legs = {"o": (own, m1, back, 0), "f": (m1, m2, back, 3), "g": (m2, m3, back, 6), "h": (own, m3, forth, 9),
            "x": (own, x1, along, 12), "y": (x1, x2, along, 15)}

    def send(leg, part):
        src, dst, device, sem = legs[leg]
        piece = pl.ds(*PARTS[part])
        go(remote(src.at[piece], dst.at[piece], q_send.at[sem + part], q_recv.at[sem + part], device))

    def arrive(leg, part):
        _, dst, _, sem = legs[leg]
        landed(dst.at[pl.ds(*PARTS[part])], q_recv.at[sem + part])

    def landed(dst, recv):
        remote(dst, dst, res_send.at[0], recv, partner).wait_recv()

    meta_routes = [(9, M1, back), (9, M3, forth), (9, X1, along), (9, 10, behind), (9, P0, partner),
                   (M3, M2, forth), (10, X2, behind), (M1, P1, partner), (M3, P3, partner), (M2, P2, partner)]

    def meta_go(i):
        src, dst, device = meta_routes[i]
        go(remote(metas[src], metas[dst], meta_send.at[i], meta_recv.at[dst], device))

    def mate_copies(i):
        quarter = lax.rem(group + 1 + i, 4)
        go(remote(lab_in, xmeta.at[i], x_send.at[i, 0], x_recv.at[i, 0], mates[i]))
        go(remote(own.at[quarter], xa.at[i], x_send.at[i, 1], x_recv.at[i, 1], mates[i]))
        go(remote(halves.at[quarter], xp.at[i], x_send.at[i, 2], x_recv.at[i, 2], mates[i]))

    for i in range(5):
        meta_go(i)
    send("o", 0)
    send("x", 0)
    mate_copies(0)
    mate_copies(2)
    send("o", 1)
    send("x", 1)
    send("o", 2)
    send("x", 2)
    go(remote(own, p0, d_send.at[0], d_recv.at[0], partner))

    def share(which, first, count, slot):
        src, dst = bufs[which], bufs[which + P1]
        go(remote(src.at[pl.ds(first, count)], dst.at[pl.ds(first, count)], d_send.at[slot], d_recv.at[which + 1], partner))

    def shared_arrival(i):
        dst = (p0, p1, p2, p3)[i]
        remote(dst, dst, d_send.at[0], d_recv.at[i], partner).wait_recv()

    def make_cols(meta, i):
        for r in range(8):
            row = jnp.broadcast_to(meta[r:r + 1, :], (LANES, LANES))
            cols[i][r // 2, (r % 2) * LANES:(r % 2 + 1) * LANES, :] = row.T

    def make_rows(meta, i):
        keys = meta[0:8, :]
        floors = keys & (-RANKS)
        for r in range(8):
            lanes = slice((r % 2) * LANES, (r % 2 + 1) * LANES)
            flats[i][r // 2, 0:1, lanes] = keys[r:r + 1, :]
            flats[i][r // 2, 1:2, lanes] = floors[r:r + 1, :]

    make_cols(own_meta, 0)
    make_rows(own_meta, 9)
    own_list = pltpu.make_async_copy(own_meta.at[pl.ds(8, 8)], lists[9], list_sem.at[9])
    own_list.start()
    for acc in accs:
        acc[...] = jnp.full((8, LANES), LOW, jnp.float32)
    row_ids = lax.broadcasted_iota(jnp.int32, (8, LANES), 0)

    def update(acc, block, row):
        spread = jnp.where(lax.rem(row_ids, 2) == 0, row[:, :LANES], row[:, LANES:])
        acc[...] = jnp.where(row_ids // 2 == block, jnp.maximum(acc[...], spread), acc[...])

    def tile(abuf, acol, aacc, a, bbuf, brows, bacc, b, same=False):
        left = jnp.concatenate([abuf[c, a] for c in range(SLICES)], axis=1)
        right = jnp.concatenate([bbuf[c, b] for c in range(SLICES)], axis=1)
        similar = lax.dot_general(left, right, (((1,), (1,)), ((), ())), preferred_element_type=jnp.float32)
        akey = cols[acol][a]
        afloor = akey & (-RANKS)
        brow = brows[b]
        for_a, for_b = None, []
        for h in range(2):
            lanes = slice(h * LANES, (h + 1) * LANES)
            bkey, bfloor = brow[0:1, lanes], brow[1:2, lanes]
            value = jnp.where(afloor == bfloor, similar[:, lanes], LOW)
            later = bkey < akey
            va = jnp.where(later, value, LOW)
            vb = jnp.where(akey < bkey, value, LOW) if same else jnp.where(later, LOW, value)
            for_a = va if for_a is None else jnp.maximum(for_a, va)
            for_b.append(jnp.max(vb, axis=0, keepdims=True))
        update(aacc, a, jnp.max(for_a.T, axis=0, keepdims=True))
        update(bacc, b, jnp.concatenate(for_b, axis=1))

    def data(i):
        if i is None:
            return own, flats[9], lists[9], accs[9], me
        return bufs[i], flats[i], lists[i], accs[i], sources[i]

    def meet(ai, bi, forward=True, backward=True):
        abuf, _, alist, aacc, adev = data(ai)
        bbuf, brows, blist, bacc, bdev = data(bi)
        col = 0 if ai is None else ai + 1

        if forward:
            tile(abuf, col, aacc, alist[0, bdev], bbuf, brows, bacc, blist[1, adev])
        if backward:
            tile(abuf, col, aacc, alist[1, bdev], bbuf, brows, bacc, blist[0, adev])

    def local(lo, hi):
        def some(i, carry):
            for n in range(5):
                v = i * 5 + n
                k = jnp.where(v >= 4, 1, 0) + jnp.where(v >= 7, 1, 0) + jnp.where(v >= 9, 1, 0)
                l = v - 3 * jnp.where(v >= 4, 1, 0) - 2 * jnp.where(v >= 7, 1, 0) - jnp.where(v >= 9, 1, 0)
                tile(own, 0, accs[9], k, own, flats[9], accs[9], l, same=True)
            return carry

        lax.fori_loop(lo, hi, some, 0)

    def have_meta(i):
        landed(metas[i], meta_recv.at[i])

    def list_copy(i):
        return pltpu.make_async_copy(metas[i].at[pl.ds(8, 8)], lists[i], list_sem.at[i])

    def use_meta(i):
        list_copy(i).start()
        make_rows(metas[i], i)
        if i < 3:
            make_cols(metas[i], i + 1)

    def set_source(points, extra):
        for b in range(4):
            rhs[b * BLOCK:(b + 1) * BLOCK, :LANES] = points[b]
            keep = (lane_ids < 64) if b < 2 else (lane_ids >= 64)
            rhs[b * BLOCK:(b + 1) * BLOCK, LANES:] = jnp.where(keep, extra[b % 2].astype(jnp.float32), 0.0).astype(jnp.bfloat16)

    def add_source(label_ref, lo, hi, mode):
        labels = label_ref[...]
        ys, zs, es = (labels // 256) % 4, (labels // 64) % 4, (labels // 32) % 2
        order = (es * 2048 + jnp.where(es == 0, zs, ys) * 512 + jnp.where(es == 0, ys, zs) * 128 + (labels // 1024) * 32
                 + labels % 32)

        def chunk(i, carry):
            m = lax.rem(i + 2 * other, 4)
            ids = lax.broadcasted_iota(jnp.int32, (ROWS, LANES), 0) + m * ROWS
            hot = jnp.concatenate(
                [jnp.where(order[r:r + 1, :] == ids, 1.0, 0.0).astype(jnp.bfloat16) for r in range(8)], axis=1)
            total = jnp.dot(hot, rhs[...], preferred_element_type=jnp.float32)
            if mode != "first":
                total = total + sums[m]
            if mode != "last":
                sums[m] = total
            else:
                extra = total[:, LANES:]
                extra = extra + pltpu.roll(extra, 64, 1)
                for b in range(32):
                    place_ = (m // 2, 2 * lax.rem(m, 2) + b // 16, (b // 4) % 4, b % 4)
                    cores[(*place_, slice(0, 32))] = total[b * 32:b * 32 + 32, :LANES]
                    cores[(*place_, slice(32, 48))] = jnp.where(
                        lane_ids[:16] < 64, extra[b * 32:b * 32 + 16], extra[b * 32 + 16:b * 32 + 32])
            return carry

        lax.fori_loop(lo, hi, chunk, 0)

    def ring(i):
        return lax.rem(main + i, 4)

    def centroid_send(src, dst, i, device):
        go(remote(src, dst, c_send.at[i], c_recv.at[i], device))

    def finish_centroids():
        quarters = [in_x[lax.rem(group - q + 4, 4)] for q in range(4)]
        tiles = [quarters[q][0:32] for q in range(4)]
        low = lane_ids[:16] < 64
        for t in range(2):
            even, odd = quarters[2 * t][32:48], quarters[2 * t + 1][32:48]
            tiles.append(jnp.concatenate([jnp.where(low, even, pltpu.roll(odd, 64, 1)),
                                          jnp.where(low, pltpu.roll(even, 64, 1), odd)], axis=0))
        squares = tiles[0] * tiles[0]
        for tile_values in tiles[1:]:
            squares = squares + tile_values * tile_values
        scale = lax.rsqrt(jnp.sum(squares, axis=-1, keepdims=True) / 768.0 + 1e-06)
        for c in range(SLICES):
            centroids_out[:, c * LANES:(c + 1) * LANES] = tiles[c] * scale

    def give_back(i):
        go(remote(accs[i], result_in.at[i], res_send.at[i], res_recv.at[i], at(sources[i])))

    def source(i):
        landed(xmeta.at[i], x_recv.at[i, 0])
        landed(xa.at[i], x_recv.at[i, 1])
        landed(xp.at[i], x_recv.at[i, 2])
        set_source(xa.at[i], xp.at[i])

    own_list.wait()
    have_meta(M3)
    meta_go(5)
    have_meta(10)
    meta_go(6)
    have_meta(M1)
    meta_go(7)
    meta_go(8)
    set_source(own.at[group], halves.at[group])
    add_source(lab_in, 0, 4, "first")
    have_meta(M2)
    meta_go(9)
    for i in (X1, X2, P0, P1, P3):
        have_meta(i)
    for i in (M1, M2, M3, X1, X2, P0, P1, P3):
        use_meta(i)
    arrive("o", 0)
    send("f", 0)
    arrive("x", 0)
    send("y", 0)
    send("h", 2)
    mate_copies(1)
    have_meta(P2)
    use_meta(P2)
    local(0, 2)
    source(0)
    add_source(xmeta.at[0], 0, 4, "add")
    source(2)
    add_source(xmeta.at[2], 0, 4, "add")
    arrive("o", 1)
    send("f", 1)
    arrive("f", 0)
    send("g", 0)
    arrive("x", 1)
    send("y", 1)
    for i in range(9):
        list_copy(i).wait()
    source(1)
    add_source(xmeta.at[1], 0, 2, "last")
    centroid_send(cores.at[other], from_core, 0, partner)
    add_source(xmeta.at[1], 2, 4, "last")
    arrive("o", 2)
    send("f", 2)
    share(M1, 0, 6, 1)
    arrive("x", 2)
    send("y", 2)
    shared_arrival(0)
    meet(None, P0, backward=False)
    meet(M1, P0, backward=False)
    meet(None, M1)
    landed(from_core, c_recv.at[0])
    for i in range(4):
        cores[core, i] = cores[core, i] + from_core[i]
    centroid_send(cores.at[core, ring(2), pl.ds(0, 2)], in_f, 1, forth)
    centroid_send(cores.at[core, ring(2), pl.ds(2, 2)], in_b, 2, back)
    meet(None, X1)
    meet(M1, X1)
    arrive("f", 1)
    send("g", 1)
    shared_arrival(1)
    meet(None, P1, backward=False)
    meet(M1, P1, backward=False)
    arrive("y", 0)
    landed(in_f, c_recv.at[1])
    cores[core, ring(1), 0:2] = cores[core, ring(1), 0:2] + in_f[...]
    centroid_send(cores.at[core, ring(1)], in2_f, 3, forth)
    landed(in_b, c_recv.at[2])
    cores[core, ring(3), 2:4] = cores[core, ring(3), 2:4] + in_b[...]
    centroid_send(cores.at[core, ring(3)], in2_b, 4, back)
    arrive("h", 2)
    share(M3, 3, 3, 3)
    arrive("g", 0)
    share(M3, 0, 1, 4)
    arrive("y", 1)
    arrive("f", 2)
    share(M2, 0, 6, 2)
    meet(None, M2, forward=False)
    meet(M2, X1)
    meet(M2, P0, backward=False)
    meet(M2, P1, backward=False)
    landed(in2_f, c_recv.at[3])
    landed(in2_b, c_recv.at[4])
    cores[core, main] = cores[core, main] + in2_f[...] + in2_b[...]
    for i, device in ((1, along), (2, across), (3, behind)):
        centroid_send(cores.at[core, main, lax.rem(side + i, 4)], in_side.at[i], 4 + i, device)
    shared_arrival(2)
    meet(None, P2, backward=False)
    meet(M1, P2, backward=False)
    meet(M2, P2, backward=False)
    arrive("y", 2)
    meet(None, X2, forward=False)
    meet(M1, X2, forward=False)
    meet(M2, X2, forward=False)
    for i in (1, 2, 3):
        landed(in_side.at[i], c_recv.at[4 + i])
    in_side[0] = cores[core, main, side] + in_side[1] + in_side[2] + in_side[3]
    in_x[0] = in_side[0, group]
    for i in (1, 2, 3):
        centroid_send(in_side.at[0, lax.rem(group + i, 4)], in_x.at[i], 7 + i, mates[i - 1])
    arrive("g", 1)
    share(M3, 1, 2, 5)
    for i in (X2, X1):
        meet(M3, i, forward=i == X1)
    for i in (P0, P1, P2):
        meet(M3, i, backward=False)
    for i in (X2, X1, P0, P1, P2):
        give_back(i)
    shared_arrival(3)
    for i in (M3, M2, M1, None):
        meet(i, P3, backward=False)
    for i in (M3, P3, M2, M1):
        give_back(i)

    for i in (1, 2, 3):
        landed(in_x.at[i], c_recv.at[7 + i])
    finish_centroids()
    best = jnp.maximum(accs[9][...], 0.0)
    for i in range(9):
        remote(result_in.at[i], result_in.at[i], res_send.at[i], res_recv.at[i], partner).wait_recv()
        best = jnp.maximum(best, result_in[i])
    scores_out[...] = best
    for copy in started:
        copy.wait_send()


def exchange(embeddings, labels, ranking, send_list, pair_list):
    dataset = pltpu.VMEM((SLICES, 4, BLOCK, LANES), jnp.bfloat16)
    dma = pltpu.SemaphoreType.DMA
    f32, bf16, i32 = jnp.float32, jnp.bfloat16, jnp.int32
    return pl.pallas_call(
        kernel,
        out_shape=(jax.ShapeDtypeStruct((8, LANES), f32), jax.ShapeDtypeStruct((32, SLICES * LANES), f32)),
        in_specs=[pl.BlockSpec(memory_space=pl.ANY)] + [pl.BlockSpec(memory_space=pltpu.VMEM)] * 4,
        out_specs=(pl.BlockSpec(memory_space=pltpu.VMEM), pl.BlockSpec(memory_space=pltpu.VMEM)),
        scratch_shapes=[dataset] * 10
        + [pltpu.VMEM((16, LANES), i32)] * 11
        + [pltpu.SMEM((8, LANES), i32)] * 10
        + [pltpu.VMEM((4, BLOCK, LANES), i32)] * 4
        + [pltpu.VMEM((8, LANES), f32)] * 10
        + [pltpu.VMEM((4, 8, BLOCK), i32)] * 10
        + [pltpu.VMEM((9, 8, LANES), f32),
           pltpu.VMEM((4, 2, BLOCK, LANES), bf16),
           pltpu.VMEM((3, 4, BLOCK, LANES), bf16),
           pltpu.VMEM((3, 2, BLOCK, LANES), bf16),
           pltpu.VMEM((3, 8, LANES), i32),
           pltpu.VMEM((ROWS, 2 * LANES), bf16),
           pltpu.VMEM((4, ROWS, 2 * LANES), f32),
           pltpu.VMEM((2, 4, 4, 4, 48, LANES), f32),
           pltpu.VMEM((4, 4, 4, 48, LANES), f32),
           pltpu.VMEM((2, 4, 48, LANES), f32),
           pltpu.VMEM((2, 4, 48, LANES), f32),
           pltpu.VMEM((4, 4, 48, LANES), f32),
           pltpu.VMEM((4, 4, 48, LANES), f32),
           pltpu.VMEM((4, 4, 48, LANES), f32),
           pltpu.VMEM((4, 48, LANES), f32),
           dma((18,)), dma((18,)), dma((6,)), dma((4,)),
           dma((10,)), dma((11,)), dma((10,)), dma((9,)), dma((9,)), dma((3, 3)), dma((3, 3)), dma((11,)), dma((11,)),
           pltpu.VMEM((ROWS, SLICES * LANES), bf16), dma((1,))],
        compiler_params=pltpu.CompilerParams(collective_id=0, has_side_effects=True, vmem_limit_bytes=60 * 1024 * 1024),
    )(embeddings, labels.reshape(8, LANES), ranking.reshape(8, LANES), send_list, pair_list)


def body(embeddings, labels, ranking, send_list, pair_list):
    scores, centroids = exchange(embeddings, labels, ranking, send_list, pair_list)
    return (scores.reshape(ROWS), centroids)


def solution(mesh):
    return jax.shard_map(
        body,
        mesh=mesh,
        in_specs=(
            P(("group", "dev"), None),
            P(("group", "dev")),
            P(("group", "dev")),
            P(("group", "dev"), None),
            P(("group", "dev"), None),
        ),
        out_specs=(P(("group", "dev")), P(("group", "dev"), None)),
        check_vma=False,
    )
```

time: 94 us -> 75.6 us (0.80); the launches traced: 92.2 us -> 75.4 us
  Pallas kernels: 88.8 us -> 71.9 us
    pallas_call x1, Pallas kernels: 88.8 us -> 71.9 us  [exchange(): pl.pallas_call(kernel, out_shape=(jax.ShapeDtypeStruct((8, LANES), f32),...]
where the time goes in v3:
time: 75.6 us; the launch traced here: 75.4 us
  Pallas kernels  71.9 us (95%)
  local copies, waits for them, and re-layouts  2.81 us (4%)
    pallas_call x1, Pallas kernels, exchange(): pl.pallas_call(kernel, out_shape=(jax.ShapeDtypeStruct((8, LANES), f32),...  71.9 us
    unnamed x2, local copies, waits for them, and re-layouts  2.81 us

profile of v3, /device:TPU:0, one launch (start us, length us, event | category | flops | bytes accessed | tf_op | source)
XLA Modules:
  0.0 75.4 jit_solution(5898855937932541134)
XLA Ops:
  0.6 71.9 %shard_map.68 = (f32[8,128]{1,0:T(8,128)}, f32[32,768]{1,0:T(8,128)}) custom-call(bf16[1024,768]{1,0:T(8,128)(2,1)} %emb_in.1, s32[8,128]{1,0:T(8,128)} %bitcast.3, s32[8,128]{1,0:T(8,128)} %bitcast.4, s32[1,32]{1,0:T(1,128)} %send_in.1, s32[1,32]{1,0:T(1,128)} %pair_in.1), custom_call_target="tpu_custom_call" | custom-call | tf_op jit(solution)/shard_map/pallas_call | solution.py:422
  72.6 1.3 %copy.9 = f32[1024]{0:T(1024)} copy(f32[1024]{0:T(1024)} %bitcast.5) | data formatting | bytes 8192
  73.8 1.5 %copy.10 = f32[32,768]{1,0:T(8,128)} copy(f32[32,768]{1,0:T(8,128)} %get-tuple-element.9) | data formatting | bytes 196608

commit v4 on v3

--- a/solution.py
+++ b/solution.py
@@ -310,89 +310,81 @@
     send("f", 0)
     arrive("x", 0)
     send("y", 0)
+    mate_copies(1)
     send("h", 2)
-    mate_copies(1)
     have_meta(P2)
     use_meta(P2)
     local(0, 2)
     source(0)
     add_source(xmeta.at[0], 0, 4, "add")
+    arrive("o", 1)
+    send("f", 1)
+    arrive("x", 1)
+    send("y", 1)
     source(2)
     add_source(xmeta.at[2], 0, 4, "add")
-    arrive("o", 1)
-    send("f", 1)
-    arrive("f", 0)
-    send("g", 0)
-    arrive("x", 1)
-    send("y", 1)
-    for i in range(9):
-        list_copy(i).wait()
+    arrive("o", 2)
+    send("f", 2)
+    share(M1, 0, 6, 1)
     source(1)
     add_source(xmeta.at[1], 0, 2, "last")
     centroid_send(cores.at[other], from_core, 0, partner)
     add_source(xmeta.at[1], 2, 4, "last")
-    arrive("o", 2)
-    send("f", 2)
-    share(M1, 0, 6, 1)
-    arrive("x", 2)
-    send("y", 2)
-    shared_arrival(0)
-    meet(None, P0, backward=False)
-    meet(M1, P0, backward=False)
-    meet(None, M1)
     landed(from_core, c_recv.at[0])
     for i in range(4):
         cores[core, i] = cores[core, i] + from_core[i]
     centroid_send(cores.at[core, ring(2), pl.ds(0, 2)], in_f, 1, forth)
     centroid_send(cores.at[core, ring(2), pl.ds(2, 2)], in_b, 2, back)
+    for i in range(9):
+        list_copy(i).wait()
+    shared_arrival(0)
+    meet(None, P0, backward=False)
+    meet(M1, P0, backward=False)
+    meet(None, M1)
+    arrive("x", 2)
+    send("y", 2)
+    arrive("f", 0)
+    send("g", 0)
     meet(None, X1)
     meet(M1, X1)
     arrive("f", 1)
     send("g", 1)
-    shared_arrival(1)
-    meet(None, P1, backward=False)
-    meet(M1, P1, backward=False)
+    landed(in_b, c_recv.at[2])
+    cores[core, ring(3), 2:4] = cores[core, ring(3), 2:4] + in_b[...]
+    centroid_send(cores.at[core, ring(3)], in2_b, 4, back)
     arrive("y", 0)
     landed(in_f, c_recv.at[1])
     cores[core, ring(1), 0:2] = cores[core, ring(1), 0:2] + in_f[...]
     centroid_send(cores.at[core, ring(1)], in2_f, 3, forth)
-    landed(in_b, c_recv.at[2])
-    cores[core, ring(3), 2:4] = cores[core, ring(3), 2:4] + in_b[...]
-    centroid_send(cores.at[core, ring(3)], in2_b, 4, back)
-    arrive("h", 2)
-    share(M3, 3, 3, 3)
-    arrive("g", 0)
-    share(M3, 0, 1, 4)
-    arrive("y", 1)
+    shared_arrival(1)
+    meet(None, P1, backward=False)
+    meet(M1, P1, backward=False)
     arrive("f", 2)
     share(M2, 0, 6, 2)
     meet(None, M2, forward=False)
     meet(M2, X1)
     meet(M2, P0, backward=False)
     meet(M2, P1, backward=False)
+    arrive("g", 0)
+    share(M3, 0, 1, 4)
+    arrive("y", 1)
+    arrive("h", 2)
+    share(M3, 3, 3, 3)
+    shared_arrival(2)
+    meet(None, P2, backward=False)
+    meet(M1, P2, backward=False)
+    meet(M2, P2, backward=False)
+    arrive("g", 1)
+    share(M3, 1, 2, 5)
     landed(in2_f, c_recv.at[3])
     landed(in2_b, c_recv.at[4])
     cores[core, main] = cores[core, main] + in2_f[...] + in2_b[...]
     for i, device in ((1, along), (2, across), (3, behind)):
         centroid_send(cores.at[core, main, lax.rem(side + i, 4)], in_side.at[i], 4 + i, device)
-    shared_arrival(2)
-    meet(None, P2, backward=False)
-    meet(M1, P2, backward=False)
-    meet(M2, P2, backward=False)
     arrive("y", 2)
-    meet(None, X2, forward=False)
-    meet(M1, X2, forward=False)
-    meet(M2, X2, forward=False)
-    for i in (1, 2, 3):
-        landed(in_side.at[i], c_recv.at[4 + i])
-    in_side[0] = cores[core, main, side] + in_side[1] + in_side[2] + in_side[3]
-    in_x[0] = in_side[0, group]
-    for i in (1, 2, 3):
-        centroid_send(in_side.at[0, lax.rem(group + i, 4)], in_x.at[i], 7 + i, mates[i - 1])
-    arrive("g", 1)
-    share(M3, 1, 2, 5)
-    for i in (X2, X1):
-        meet(M3, i, forward=i == X1)
+    for i in (None, M1, M2, M3):
+        meet(i, X2, forward=False)
+    meet(M3, X1)
     for i in (P0, P1, P2):
         meet(M3, i, backward=False)
     for i in (X2, X1, P0, P1, P2):
@@ -402,7 +394,12 @@
         meet(i, P3, backward=False)
     for i in (M3, P3, M2, M1):
         give_back(i)
-
+    for i in (1, 2, 3):
+        landed(in_side.at[i], c_recv.at[4 + i])
+    in_side[0] = cores[core, main, side] + in_side[1] + in_side[2] + in_side[3]
+    in_x[0] = in_side[0, group]
+    for i in (1, 2, 3):
+        centroid_send(in_side.at[0, lax.rem(group + i, 4)], in_x.at[i], 7 + i, mates[i - 1])
     for i in (1, 2, 3):
         landed(in_x.at[i], c_recv.at[7 + i])
     finish_centroids()
@@ -452,8 +449,23 @@
     )(embeddings, labels.reshape(8, LANES), ranking.reshape(8, LANES), send_list, pair_list)
 
 
+def store_kernel(scores_in, centroids_in, scores_out, centroids_out):
+    scores_out[...] = jnp.maximum(scores_in[...], 0.0)
+    centroids_out[...] = centroids_in[...]
+
+
+def store(scores, centroids):
+    return pl.pallas_call(
+        store_kernel,
+        out_shape=(jax.ShapeDtypeStruct(scores.shape, scores.dtype), jax.ShapeDtypeStruct(centroids.shape, centroids.dtype)),
+        in_specs=[pl.BlockSpec(memory_space=pltpu.VMEM)] * 2,
+        out_specs=(pl.BlockSpec(memory_space=pltpu.VMEM), pl.BlockSpec(memory_space=pltpu.VMEM)),
+    )(scores, centroids)
+
+
 def body(embeddings, labels, ranking, send_list, pair_list):
     scores, centroids = exchange(embeddings, labels, ranking, send_list, pair_list)
+    scores, centroids = store(scores, centroids)
     return (scores.reshape(ROWS), centroids)
 
 

time: 75.6 us -> 72.3 us (0.956)
  local copies, waits for them, and re-layouts: 2.81 us -> 0 us
    unnamed x2 -> x0, local copies, waits for them, and re-layouts: 2.81 us -> none
    pallas_call x1, Pallas kernels: 71.9 us -> 69.9 us  [exchange(): pl.pallas_call(kernel, out_shape=(jax.ShapeDtypeStruct((8, LANES), f32),...]
    pallas_call x0 -> x1, Pallas kernels: none -> 1.55 us  [store(): pl.pallas_call(store_kernel, out_shape=(jax.ShapeDtypeStruct(scores.shape...]
where the time goes in v4:
time: 72.3 us; the launch traced here: 72.1 us
  Pallas kernels  71.5 us (99%)
    pallas_call x1, Pallas kernels, exchange(): pl.pallas_call(kernel, out_shape=(jax.ShapeDtypeStruct((8, LANES), f32),...  69.9 us
    pallas_call x1, Pallas kernels, store(): pl.pallas_call(store_kernel, out_shape=(jax.ShapeDtypeStruct(scores.shape...  1.55 us

profile of v4, /device:TPU:0, one launch (start us, length us, event | category | flops | bytes accessed | tf_op | source)
XLA Modules:
  0.0 72.1 jit_solution(2613529778388749901)
XLA Ops:
  0.6 69.9 %shard_map.68 = (f32[8,128]{1,0:T(8,128)}, f32[32,768]{1,0:T(8,128)}) custom-call(bf16[1024,768]{1,0:T(8,128)(2,1)} %emb_in.1, s32[8,128]{1,0:T(8,128)} %bitcast.3, s32[8,128]{1,0:T(8,128)} %bitcast.4, s32[1,32]{1,0:T(1,128)} %send_in.1, s32[1,32]{1,0:T(1,128)} %pair_in.1), custom_call_target="tpu_custom_call" | custom-call | tf_op jit(solution)/shard_map/pallas_call | solution.py:419
  70.6 1.5 %shard_map.69 = (f32[8,128]{1,0:T(8,128)}, f32[32,768]{1,0:T(8,128)}) custom-call(f32[8,128]{1,0:T(8,128)} %get-tuple-element.6.scores_in, f32[32,768]{1,0:T(8,128)} %get-tuple-element.7.centroids_in), custom_call_target="tpu_custom_call" | custom-call | tf_op jit(solution)/shard_map/pallas_call | solution.py:458

commit v5 on v4

--- a/solution.py
+++ b/solution.py
@@ -17,7 +17,7 @@
 PARTS = ((0, 1), (1, 2), (3, 3))
 
 
-def kernel(emb_in, lab_in, rank_in, send_in, pair_in, scores_out, centroids_out,
+def kernel(emb_hbm, lab_hbm, rank_hbm, send_hbm, pair_hbm, scores_out, centroids_out,
            own, m1, m2, m3, x1, x2, p0, p1, p2, p3, *rest):
     metas = rest[0:11]
     lists = rest[11:21]
@@ -25,10 +25,14 @@
     accs = rest[25:35]
     flats = rest[35:45]
     own_meta = metas[9]
-    (result_in, halves, xa, xp, xmeta, rhs, sums, cores, from_core, in_f, in_b, in2_f, in2_b, in_side, in_x,
+    (result_in, halves, xa, xp, xmeta, rhs, sums, cores, from_core, in_f, in_b, in2_f, in2_b, in_last,
      q_send, q_recv, d_send, d_recv, meta_send, meta_recv, list_sem, res_send, res_recv,
-     x_send, x_recv, c_send, c_recv, emb, emb_sem) = rest[45:]
+     x_send, x_recv, c_send, c_recv, emb, lab_in, rank_in, send_in, pair_in, in_sem) = rest[45:]
     bufs = (m1, m2, m3, x1, x2, p0, p1, p2, p3)
+    loads = [pltpu.make_async_copy(src, dst, in_sem.at[i]) for i, (src, dst) in enumerate(
+        ((emb_hbm, emb), (lab_hbm, lab_in), (rank_hbm, rank_in), (send_hbm, send_in), (pair_hbm, pair_in)))]
+    for copy in loads:
+        copy.start()
     group = lax.axis_index("group")
     me = lax.axis_index("dev")
     core = lax.rem(me, 2)
@@ -51,15 +55,14 @@
     partner = at(place(side, main, other))
 
     behind = at(place(main, side + 3, core))
-    across = at(place(main, side + 2, core))
     mates = [(lax.rem(group + i, 4), me) for i in (1, 2, 3)]
 
     barrier = pltpu.get_barrier_semaphore()
     for device in [forth, back, along, behind, partner] + mates:
         pl.semaphore_signal(barrier, inc=1, device_id=device, device_id_type=MESH)
 
-    emb_copy = pltpu.make_async_copy(emb_in, emb, emb_sem.at[0])
-    emb_copy.start()
+    for copy in loads[1:]:
+        copy.wait()
     own_meta[0:8, :] = lab_in[...] * RANKS + rank_in[...]
     own_meta[8:9, 0:32] = send_in[...]
     own_meta[9:10, 0:32] = pair_in[...]
@@ -73,7 +76,7 @@
             own[c, i // 2, pl.ds(pl.multiple_of(lax.rem(i, 2) * 128, 128), 128), :] = unit[:, c * LANES:(c + 1) * LANES]
         return carry
 
-    emb_copy.wait()
+    loads[0].wait()
     lax.fori_loop(0, 8, normalize, 0)
     lane_ids = lax.broadcasted_iota(jnp.int32, (BLOCK, LANES), 1)
 
@@ -94,6 +97,11 @@
     def go(copy):
         copy.start()
         started.append(copy)
+
+    def drain(count):
+        for copy in started[:count]:
+            copy.wait_send()
+        del started[:count]
 
     legs = {"o": (own, m1, back, 0), "f": (m1, m2, back, 3), "g": (m2, m3, back, 6), "h": (own, m3, forth, 9),
             "x": (own, x1, along, 12), "y": (x1, x2, along, 15)}
@@ -266,8 +274,13 @@
     def centroid_send(src, dst, i, device):
         go(remote(src, dst, c_send.at[i], c_recv.at[i], device))
 
+    owners = sorted([(i, k) for k in range(4) for i in range(4) if i or k], key=lambda o: -(min(o[0], 4 - o[0]) + min(o[1], 4 - o[1])))
+
     def finish_centroids():
-        quarters = [in_x[lax.rem(group - q + 4, 4)] for q in range(4)]
+        quarters = []
+        for q in range(4):
+            step = lax.rem(group - q + 4, 4)
+            quarters.append(in_last[step, 0] + in_last[step, 1] + in_last[step, 2] + in_last[step, 3])
         tiles = [quarters[q][0:32] for q in range(4)]
         low = lane_ids[:16] < 64
         for t in range(2):
@@ -359,6 +372,7 @@
     shared_arrival(1)
     meet(None, P1, backward=False)
     meet(M1, P1, backward=False)
+    early = len(started) - 8
     arrive("f", 2)
     share(M2, 0, 6, 2)
     meet(None, M2, forward=False)
@@ -374,42 +388,39 @@
     meet(None, P2, backward=False)
     meet(M1, P2, backward=False)
     meet(M2, P2, backward=False)
+    drain(early)
     arrive("g", 1)
     share(M3, 1, 2, 5)
     landed(in2_f, c_recv.at[3])
     landed(in2_b, c_recv.at[4])
     cores[core, main] = cores[core, main] + in2_f[...] + in2_b[...]
-    for i, device in ((1, along), (2, across), (3, behind)):
-        centroid_send(cores.at[core, main, lax.rem(side + i, 4)], in_side.at[i], 4 + i, device)
+    in_last[0, 0] = cores[core, main, side, group]
+    for i, k in owners:
+        target = lax.rem(group + i, 4), lax.rem(side + k, 4)
+        centroid_send(cores.at[core, main, target[1], target[0]], in_last.at[i, k], 4 * i + k + 4,
+                      (target[0], place(main, side + k, core)))
     arrive("y", 2)
     for i in (None, M1, M2, M3):
         meet(i, X2, forward=False)
     meet(M3, X1)
     for i in (P0, P1, P2):
         meet(M3, i, backward=False)
-    for i in (X2, X1, P0, P1, P2):
+    for i in (X2, P2, P1, X1, P0):
         give_back(i)
     shared_arrival(3)
     for i in (M3, M2, M1, None):
         meet(i, P3, backward=False)
-    for i in (M3, P3, M2, M1):
+    for i in (M2, P3, M1, M3):
         give_back(i)
-    for i in (1, 2, 3):
-        landed(in_side.at[i], c_recv.at[4 + i])
-    in_side[0] = cores[core, main, side] + in_side[1] + in_side[2] + in_side[3]
-    in_x[0] = in_side[0, group]
-    for i in (1, 2, 3):
-        centroid_send(in_side.at[0, lax.rem(group + i, 4)], in_x.at[i], 7 + i, mates[i - 1])
-    for i in (1, 2, 3):
-        landed(in_x.at[i], c_recv.at[7 + i])
+    for i, k in owners:
+        landed(in_last.at[i, k], c_recv.at[4 * i + k + 4])
     finish_centroids()
     best = jnp.maximum(accs[9][...], 0.0)
     for i in range(9):
         remote(result_in.at[i], result_in.at[i], res_send.at[i], res_recv.at[i], partner).wait_recv()
         best = jnp.maximum(best, result_in[i])
     scores_out[...] = best
-    for copy in started:
-        copy.wait_send()
+    drain(len(started))
 
 
 def exchange(embeddings, labels, ranking, send_list, pair_list):
@@ -419,7 +430,7 @@
     return pl.pallas_call(
         kernel,
         out_shape=(jax.ShapeDtypeStruct((8, LANES), f32), jax.ShapeDtypeStruct((32, SLICES * LANES), f32)),
-        in_specs=[pl.BlockSpec(memory_space=pl.ANY)] + [pl.BlockSpec(memory_space=pltpu.VMEM)] * 4,
+        in_specs=[pl.BlockSpec(memory_space=pl.ANY)] * 5,
         out_specs=(pl.BlockSpec(memory_space=pltpu.VMEM), pl.BlockSpec(memory_space=pltpu.VMEM)),
         scratch_shapes=[dataset] * 10
         + [pltpu.VMEM((16, LANES), i32)] * 11
@@ -441,10 +452,10 @@
            pltpu.VMEM((4, 4, 48, LANES), f32),
            pltpu.VMEM((4, 4, 48, LANES), f32),
            pltpu.VMEM((4, 4, 48, LANES), f32),
-           pltpu.VMEM((4, 48, LANES), f32),
            dma((18,)), dma((18,)), dma((6,)), dma((4,)),
-           dma((10,)), dma((11,)), dma((10,)), dma((9,)), dma((9,)), dma((3, 3)), dma((3, 3)), dma((11,)), dma((11,)),
-           pltpu.VMEM((ROWS, SLICES * LANES), bf16), dma((1,))],
+           dma((10,)), dma((11,)), dma((10,)), dma((9,)), dma((9,)), dma((3, 3)), dma((3, 3)), dma((20,)), dma((20,)),
+           pltpu.VMEM((ROWS, SLICES * LANES), bf16), pltpu.VMEM((8, LANES), i32), pltpu.VMEM((8, LANES), i32),
+           pltpu.VMEM((1, 32), i32), pltpu.VMEM((1, 32), i32), dma((5,))],
         compiler_params=pltpu.CompilerParams(collective_id=0, has_side_effects=True, vmem_limit_bytes=60 * 1024 * 1024),
     )(embeddings, labels.reshape(8, LANES), ranking.reshape(8, LANES), send_list, pair_list)
 

time: 72.3 us -> 68.9 us (0.953)
  Pallas kernels: 71.5 us -> 68 us
    pallas_call x1, Pallas kernels: 69.9 us -> 66.5 us  [exchange(): pl.pallas_call(kernel, out_shape=(jax.ShapeDtypeStruct((8, LANES), f32),...]
where the time goes in v5:
time: 68.9 us; the launch traced here: 68.7 us
  Pallas kernels  68 us (99%)
    pallas_call x1, Pallas kernels, exchange(): pl.pallas_call(kernel, out_shape=(jax.ShapeDtypeStruct((8, LANES), f32),...  66.5 us
    pallas_call x1, Pallas kernels, store(): pl.pallas_call(store_kernel, out_shape=(jax.ShapeDtypeStruct(scores.shape...  1.55 us

profile of v5, /device:TPU:0, one launch (start us, length us, event | category | flops | bytes accessed | tf_op | source)
XLA Modules:
  0.0 68.7 jit_solution(13946459962613859276)
XLA Ops:
  0.6 66.5 %shard_map.68 = (f32[8,128]{1,0:T(8,128)}, f32[32,768]{1,0:T(8,128)}) custom-call(bf16[1024,768]{1,0:T(8,128)(2,1)} %emb_hbm.1, s32[8,128]{1,0:T(8,128)} %bitcast.3, s32[8,128]{1,0:T(8,128)} %bitcast.4, s32[1,32]{1,0:T(1,128)} %send_hbm.1, s32[1,32]{1,0:T(1,128)} %pair_hbm.1), custom_call_target="tpu_custom_call" | custom-call | tf_op jit(solution)/shard_map/pallas_call | solution.py:430
  67.1 1.5 %shard_map.69 = (f32[8,128]{1,0:T(8,128)}, f32[32,768]{1,0:T(8,128)}) custom-call(f32[8,128]{1,0:T(8,128)} %get-tuple-element.6.scores_in, f32[32,768]{1,0:T(8,128)} %get-tuple-element.7.centroids_in), custom_call_target="tpu_custom_call" | custom-call | tf_op jit(solution)/shard_map/pallas_call | solution.py:469

commit v6 on v5

--- a/solution.py
+++ b/solution.py
@@ -15,9 +15,10 @@
 MESH = pl.DeviceIdType.MESH
 M1, M2, M3, X1, X2, P0, P1, P2, P3 = range(9)
 PARTS = ((0, 1), (1, 2), (3, 3))
-
-
-def kernel(emb_hbm, lab_hbm, rank_hbm, send_hbm, pair_hbm, scores_out, centroids_out,
+SIDE_ORDER = (2, 1, 3, 0)
+
+
+def kernel(emb_hbm, lab_hbm, rank_hbm, send_hbm, pair_hbm, scores_hbm, centroids_hbm,
            own, m1, m2, m3, x1, x2, p0, p1, p2, p3, *rest):
     metas = rest[0:11]
     lists = rest[11:21]
@@ -27,7 +28,8 @@
     own_meta = metas[9]
     (result_in, halves, xa, xp, xmeta, rhs, sums, cores, from_core, in_f, in_b, in2_f, in2_b, in_last,
      q_send, q_recv, d_send, d_recv, meta_send, meta_recv, list_sem, res_send, res_recv,
-     x_send, x_recv, c_send, c_recv, emb, lab_in, rank_in, send_in, pair_in, in_sem) = rest[45:]
+     x_send, x_recv, c_send, c_recv, emb, lab_in, rank_in, send_in, pair_in, in_sem,
+     scores_out, centroids_out, out_sem) = rest[45:]
     bufs = (m1, m2, m3, x1, x2, p0, p1, p2, p3)
     loads = [pltpu.make_async_copy(src, dst, in_sem.at[i]) for i, (src, dst) in enumerate(
         ((emb_hbm, emb), (lab_hbm, lab_in), (rank_hbm, rank_in), (send_hbm, send_in), (pair_hbm, pair_in)))]
@@ -275,6 +277,21 @@
         go(remote(src, dst, c_send.at[i], c_recv.at[i], device))
 
     owners = sorted([(i, k) for k in range(4) for i in range(4) if i or k], key=lambda o: -(min(o[0], 4 - o[0]) + min(o[1], 4 - o[1])))
+
+    def across(k):
+        return lax.rem(side + k, 4)
+
+    def to_owners(k):
+        landed(in2_f.at[across(k)], c_recv.at[20 + k])
+        landed(in2_b.at[across(k)], c_recv.at[24 + k])
+        mine = cores.at[core, main, across(k)]
+        mine[...] = mine[...] + in2_f[across(k)] + in2_b[across(k)]
+        if k == 0:
+            in_last[0, 0] = mine[group]
+        for i in (2, 1, 3, 0):
+            if i or k:
+                target = lax.rem(group + i, 4)
+                centroid_send(mine.at[target], in_last.at[i, k], 4 * i + k + 4, (target, place(main, side + k, core)))
 
     def finish_centroids():
         quarters = []
@@ -364,11 +381,13 @@
     send("g", 1)
     landed(in_b, c_recv.at[2])
     cores[core, ring(3), 2:4] = cores[core, ring(3), 2:4] + in_b[...]
-    centroid_send(cores.at[core, ring(3)], in2_b, 4, back)
+    for k in SIDE_ORDER:
+        centroid_send(cores.at[core, ring(3), across(k)], in2_b.at[across(k)], 24 + k, back)
     arrive("y", 0)
     landed(in_f, c_recv.at[1])
     cores[core, ring(1), 0:2] = cores[core, ring(1), 0:2] + in_f[...]
-    centroid_send(cores.at[core, ring(1)], in2_f, 3, forth)
+    for k in SIDE_ORDER:
+        centroid_send(cores.at[core, ring(1), across(k)], in2_f.at[across(k)], 20 + k, forth)
     shared_arrival(1)
     meet(None, P1, backward=False)
     meet(M1, P1, backward=False)
@@ -391,36 +410,39 @@
     drain(early)
     arrive("g", 1)
     share(M3, 1, 2, 5)
-    landed(in2_f, c_recv.at[3])
-    landed(in2_b, c_recv.at[4])
-    cores[core, main] = cores[core, main] + in2_f[...] + in2_b[...]
-    in_last[0, 0] = cores[core, main, side, group]
-    for i, k in owners:
-        target = lax.rem(group + i, 4), lax.rem(side + k, 4)
-        centroid_send(cores.at[core, main, target[1], target[0]], in_last.at[i, k], 4 * i + k + 4,
-                      (target[0], place(main, side + k, core)))
+    meet(M3, X1)
+    for i in (P0, P1, P2):
+        meet(M3, i, backward=False)
+    to_owners(2)
+    to_owners(1)
+    shared_arrival(3)
+    for i in (M3, M2, M1, None):
+        meet(i, P3, backward=False)
+    for i in (P2, P1, P3, X1, P0):
+        give_back(i)
+    to_owners(3)
     arrive("y", 2)
     for i in (None, M1, M2, M3):
         meet(i, X2, forward=False)
-    meet(M3, X1)
-    for i in (P0, P1, P2):
-        meet(M3, i, backward=False)
-    for i in (X2, P2, P1, X1, P0):
+    for i in (X2, M2, M1, M3):
         give_back(i)
-    shared_arrival(3)
-    for i in (M3, M2, M1, None):
-        meet(i, P3, backward=False)
-    for i in (M2, P3, M1, M3):
-        give_back(i)
+    to_owners(0)
+    drain(len(started) - 20)
     for i, k in owners:
         landed(in_last.at[i, k], c_recv.at[4 * i + k + 4])
     finish_centroids()
+    stores = [pltpu.make_async_copy(src, dst, out_sem.at[i]) for i, (src, dst) in enumerate(
+        ((centroids_out, centroids_hbm), (scores_out, scores_hbm)))]
+    stores[0].start()
+    drain(len(started))
     best = jnp.maximum(accs[9][...], 0.0)
     for i in range(9):
-        remote(result_in.at[i], result_in.at[i], res_send.at[i], res_recv.at[i], partner).wait_recv()
+        landed(result_in.at[i], res_recv.at[i])
         best = jnp.maximum(best, result_in[i])
     scores_out[...] = best
-    drain(len(started))
+    stores[1].start()
+    for copy in stores:
+        copy.wait()
 
 
 def exchange(embeddings, labels, ranking, send_list, pair_list):
@@ -431,7 +453,7 @@
         kernel,
         out_shape=(jax.ShapeDtypeStruct((8, LANES), f32), jax.ShapeDtypeStruct((32, SLICES * LANES), f32)),
         in_specs=[pl.BlockSpec(memory_space=pl.ANY)] * 5,
-        out_specs=(pl.BlockSpec(memory_space=pltpu.VMEM), pl.BlockSpec(memory_space=pltpu.VMEM)),
+        out_specs=(pl.BlockSpec(memory_space=pl.ANY), pl.BlockSpec(memory_space=pl.ANY)),
         scratch_shapes=[dataset] * 10
         + [pltpu.VMEM((16, LANES), i32)] * 11
         + [pltpu.SMEM((8, LANES), i32)] * 10
@@ -453,9 +475,10 @@
            pltpu.VMEM((4, 4, 48, LANES), f32),
            pltpu.VMEM((4, 4, 48, LANES), f32),
            dma((18,)), dma((18,)), dma((6,)), dma((4,)),
-           dma((10,)), dma((11,)), dma((10,)), dma((9,)), dma((9,)), dma((3, 3)), dma((3, 3)), dma((20,)), dma((20,)),
+           dma((10,)), dma((11,)), dma((10,)), dma((9,)), dma((9,)), dma((3, 3)), dma((3, 3)), dma((28,)), dma((28,)),
            pltpu.VMEM((ROWS, SLICES * LANES), bf16), pltpu.VMEM((8, LANES), i32), pltpu.VMEM((8, LANES), i32),
-           pltpu.VMEM((1, 32), i32), pltpu.VMEM((1, 32), i32), dma((5,))],
+           pltpu.VMEM((1, 32), i32), pltpu.VMEM((1, 32), i32), dma((5,)),
+           pltpu.VMEM((8, LANES), f32), pltpu.VMEM((32, SLICES * LANES), f32), dma((2,))],
         compiler_params=pltpu.CompilerParams(collective_id=0, has_side_effects=True, vmem_limit_bytes=60 * 1024 * 1024),
     )(embeddings, labels.reshape(8, LANES), ranking.reshape(8, LANES), send_list, pair_list)
 

time: 68.9 us -> 67.8 us (0.984)
  Pallas kernels: 68 us -> 67 us
    pallas_call x1, Pallas kernels: 66.5 us -> 65.5 us  [exchange(): pl.pallas_call(kernel, out_shape=(jax.ShapeDtypeStruct((8, LANES), f32),...]
where the time goes in v6:
time: 67.8 us; the launch traced here: 67.7 us
  Pallas kernels  67 us (99%)
    pallas_call x1, Pallas kernels, exchange(): pl.pallas_call(kernel, out_shape=(jax.ShapeDtypeStruct((8, LANES), f32),...  65.5 us
    pallas_call x1, Pallas kernels, store(): pl.pallas_call(store_kernel, out_shape=(jax.ShapeDtypeStruct(scores.shape...  1.55 us

profile of v6, /device:TPU:0, one launch (start us, length us, event | category | flops | bytes accessed | tf_op | source)
XLA Modules:
  0.0 67.7 jit_solution(11198589481147259948)
XLA Ops:
  0.6 65.5 %shard_map.68 = (f32[8,128]{1,0:T(8,128)}, f32[32,768]{1,0:T(8,128)}) custom-call(bf16[1024,768]{1,0:T(8,128)(2,1)} %emb_hbm.1, s32[8,128]{1,0:T(8,128)} %bitcast.3, s32[8,128]{1,0:T(8,128)} %bitcast.4, s32[1,32]{1,0:T(1,128)} %send_hbm.1, s32[1,32]{1,0:T(1,128)} %pair_hbm.1), custom_call_target="tpu_custom_call" | custom-call | tf_op jit(solution)/shard_map/pallas_call | solution.py:452
  66.1 1.5 %shard_map.69 = (f32[8,128]{1,0:T(8,128)}, f32[32,768]{1,0:T(8,128)}) custom-call(f32[8,128]{1,0:T(8,128)} %get-tuple-element.6.scores_in, f32[32,768]{1,0:T(8,128)} %get-tuple-element.7.centroids_in), custom_call_target="tpu_custom_call" | custom-call | tf_op jit(solution)/shard_map/pallas_call | solution.py:492

commit v7 on v6

--- a/solution.py
+++ b/solution.py
@@ -15,7 +15,7 @@
 MESH = pl.DeviceIdType.MESH
 M1, M2, M3, X1, X2, P0, P1, P2, P3 = range(9)
 PARTS = ((0, 1), (1, 2), (3, 3))
-SIDE_ORDER = (2, 1, 3, 0)
+SIDE_ORDER = (1, 2, 3, 0)
 
 
 def kernel(emb_hbm, lab_hbm, rank_hbm, send_hbm, pair_hbm, scores_hbm, centroids_hbm,
@@ -354,7 +354,6 @@
     source(2)
     add_source(xmeta.at[2], 0, 4, "add")
     arrive("o", 2)
-    send("f", 2)
     share(M1, 0, 6, 1)
     source(1)
     add_source(xmeta.at[1], 0, 2, "last")
@@ -365,6 +364,7 @@
         cores[core, i] = cores[core, i] + from_core[i]
     centroid_send(cores.at[core, ring(2), pl.ds(0, 2)], in_f, 1, forth)
     centroid_send(cores.at[core, ring(2), pl.ds(2, 2)], in_b, 2, back)
+    send("f", 2)
     for i in range(9):
         list_copy(i).wait()
     shared_arrival(0)
@@ -413,8 +413,8 @@
     meet(M3, X1)
     for i in (P0, P1, P2):
         meet(M3, i, backward=False)
+    to_owners(1)
     to_owners(2)
-    to_owners(1)
     shared_arrival(3)
     for i in (M3, M2, M1, None):
         meet(i, P3, backward=False)

time: 67.8 us -> 67.8 us (level)
  no operation moved by 1% of the time
where the time goes in v7:
time: 67.8 us; the launch traced here: 67.7 us
  Pallas kernels  67 us (99%)
    pallas_call x1, Pallas kernels, exchange(): pl.pallas_call(kernel, out_shape=(jax.ShapeDtypeStruct((8, LANES), f32),...  65.5 us
    pallas_call x1, Pallas kernels, store(): pl.pallas_call(store_kernel, out_shape=(jax.ShapeDtypeStruct(scores.shape...  1.55 us

profile of v7, /device:TPU:0, one launch (start us, length us, event | category | flops | bytes accessed | tf_op | source)
XLA Modules:
  0.0 67.7 jit_solution(7350938585871709139)
XLA Ops:
  0.6 65.5 %shard_map.68 = (f32[8,128]{1,0:T(8,128)}, f32[32,768]{1,0:T(8,128)}) custom-call(bf16[1024,768]{1,0:T(8,128)(2,1)} %emb_hbm.1, s32[8,128]{1,0:T(8,128)} %bitcast.3, s32[8,128]{1,0:T(8,128)} %bitcast.4, s32[1,32]{1,0:T(1,128)} %send_hbm.1, s32[1,32]{1,0:T(1,128)} %pair_hbm.1), custom_call_target="tpu_custom_call" | custom-call | tf_op jit(solution)/shard_map/pallas_call | solution.py:452
  66.1 1.5 %shard_map.69 = (f32[8,128]{1,0:T(8,128)}, f32[32,768]{1,0:T(8,128)}) custom-call(f32[8,128]{1,0:T(8,128)} %get-tuple-element.6.scores_in, f32[32,768]{1,0:T(8,128)} %get-tuple-element.7.centroids_in), custom_call_target="tpu_custom_call" | custom-call | tf_op jit(solution)/shard_map/pallas_call | solution.py:492
